TPU v7x, 32 devices: a whole 2x2x4 slice. The times are simulated.
32 devices in a mesh: dp: 2 (over core), blk: 16 (over z, y, x).
Axes of the slice: x: 2, y: 2, z: 4, core: 2. Of those that a mesh axis runs over, the one named last changes fastest.
Arguments:
- tokens: bfloat16 [2, 4096, 768], P('dp', 'blk'), may hold values from -6 to 6
- positions: int32 [2, 4096], P('dp', 'blk'), may hold values from 0 to 4095, as said below
- gain_attention: bfloat16 [768], P(('dp', 'blk')), may hold values from 0.5 to 1.5
- bias_attention: bfloat16 [768], P(('dp', 'blk')), may hold values from -1.5 to 1.5
- gain_feed: bfloat16 [768], P(('dp', 'blk')), may hold values from 0.5 to 1.5
- bias_feed: bfloat16 [768], P(('dp', 'blk')), may hold values from -1.5 to 1.5
- weight_joined: bfloat16 [768, 2304], P(('dp', 'blk')), may hold values from -0.3125 to 0.3125
- bias_joined: bfloat16 [2304], P(('dp', 'blk')), may hold values from -3 to 3
- weight_merge: bfloat16 [768, 768], P(('dp', 'blk')), may hold values from -0.875 to 0.875
- bias_merge: bfloat16 [768], P(('dp', 'blk')), may hold values from -1.5 to 1.5
- weight_expand: bfloat16 [768, 3072], P(('dp', 'blk')), may hold values from -0.21875 to 0.21875
- bias_expand: bfloat16 [3072], P(('dp', 'blk')), may hold values from -3 to 3
- weight_reduce: bfloat16 [3072, 768], P(('dp', 'blk')), may hold values from -0.109375 to 0.109375
- bias_reduce: bfloat16 [768], P(('dp', 'blk')), may hold values from -1.5 to 1.5
- cotangent: bfloat16 [2, 4096, 768], P('dp', 'blk'), may hold values from -6 to 6
Outputs:
- result: bfloat16 [2, 4096, 768], P('dp', 'blk')
- gradient_tokens: float32 [2, 4096, 768], P('dp', 'blk')
- gradient_gain_attention: float32 [768], P(('dp', 'blk'))
- gradient_bias_attention: float32 [768], P(('dp', 'blk'))
- gradient_gain_feed: float32 [768], P(('dp', 'blk'))
- gradient_bias_feed: float32 [768], P(('dp', 'blk'))
- gradient_weight_joined: float32 [768, 2304], P(('dp', 'blk'))
- gradient_bias_joined: float32 [2304], P(('dp', 'blk'))
- gradient_weight_merge: float32 [768, 768], P(('dp', 'blk'))
- gradient_bias_merge: float32 [768], P(('dp', 'blk'))
- gradient_weight_expand: float32 [768, 3072], P(('dp', 'blk'))
- gradient_bias_expand: float32 [3072], P(('dp', 'blk'))
- gradient_weight_reduce: float32 [3072, 768], P(('dp', 'blk'))
- gradient_bias_reduce: float32 [768], P(('dp', 'blk'))
Inputs may be any that keep to these rules, and one draw needn't show every extreme that they name: Each row is a permutation of the positions of one sequence, made of runs of 128 ascending consecutive positions, each run starting at a multiple of 128.
All inputs are finite; a program needn't handle non-finite values.
Results may differ from a plain program's by a relative error of at most 0.014.
Values may be sent and summed in bfloat16 or wider, within the bound.
No kernel may reach another device: no remote copies, remote signals or barrier semaphores. Data moves between devices by JAX's collectives and lax.ppermute only.
A program may use at most 128 MiB of HBM per device.

v0:
```python
import functools
import math

import jax
import jax.numpy as jnp
from jax import lax
from jax.experimental import pallas as pl
from jax.experimental.pallas import tpu as pltpu
from jax.sharding import PartitionSpec as P

HD = 64
ROT = 16
TP = 4
RUN = 128
TILE = 2 * RUN
FORWARD_KEYS, FORWARD_REST = 1024, 1024
BACKWARD_KEYS, BACKWARD_REST = 1024, 512
VMEM = 56 * 2**20

norm_eps = 1e-05
masked_score = -1e30
low = jnp.bfloat16
full = jnp.float32


def dot(a, b, dims=((1,), (0,))):
    return lax.dot_general(a, b, (dims, ((), ())), preferred_element_type=full)


def tile_of(tile, q_runs_ref, q_order_ref):
    early, late = q_order_ref[2 * tile], q_order_ref[2 * tile + 1]
    early_run, late_run = q_runs_ref[early], q_runs_ref[late]
    rows = [pl.ds(pl.multiple_of(run * RUN, RUN), RUN) for run in (early, late)]
    column = lax.broadcasted_iota(jnp.int32, (1, TILE), 1)
    places = jnp.where(column < RUN, early_run * RUN + column, late_run * RUN + column - RUN)
    return rows, places, early_run * RUN, late_run * RUN + RUN


def over_keys(step, by_all, by_some, many, few, carry):
    blocks = lax.div(by_all, many)
    carry = lax.fori_loop(0, blocks, functools.partial(step, False, many), carry)
    first = blocks * (many // few)
    last = lax.div(by_some + few - 1, few)
    return lax.fori_loop(first, last, functools.partial(step, True, few), carry)


def columns_of(ref, rows, part=slice(None)):
    return jnp.concatenate([ref[part, at] for at in rows], axis=1)


def hidden(scores, first, places):
    k_places = first + lax.broadcasted_iota(jnp.int32, scores.shape, 0)
    return jnp.where(k_places <= places, scores, masked_score)


def forward_kernel(
    heads, groups, runs, q_runs_ref, q_order_ref, k_runs_ref, q_ref, o_grad_ref, *refs
):
    merge_ref, fed_ref, *kv_refs = refs[: groups + 2]
    out_ref, kv, kv_turned, log_ref, delta_ref, *branch_refs = refs[groups + 2 : -3]
    first_w, state, out_total = refs[-3:]
    pair = 2 * HD

    for source in range(groups):

        def place(run, carry, source=source):
            at = pl.multiple_of(k_runs_ref[source * runs + run] * RUN, RUN)
            columns = kv_refs[source][:, pl.ds(pl.multiple_of(run * RUN, RUN), RUN)]
            kv_turned[:, pl.ds(at, RUN)] = columns
            for head in range(heads):
                part = slice(head * pair, (head + 1) * pair)
                kv[pl.ds(at, RUN), part] = columns[part, :].T
            return carry

        lax.fori_loop(0, runs, place, 0)

    def tile_step(tile, carry):
        rows, places, by_all, by_some = tile_of(tile, q_runs_ref, q_order_ref)
        nothing = jnp.zeros((HD, TILE), low)
        for head in range(heads):
            part = slice(head * HD, (head + 1) * HD)
            first_w[head] = jnp.concatenate([columns_of(q_ref, rows, part), nothing], axis=0)
        state[...] = jnp.full(state.shape, masked_score, full)
        out_total[...] = jnp.zeros_like(out_total)

        def step(hides, size, block, sums):
            at = pl.ds(pl.multiple_of(block * size, size), size)
            new_sums = []
            products = [
                dot(kv[at, head * pair : (head + 1) * pair], first_w[head]) for head in range(heads)
            ]
            for head in range(heads):
                scores = products[head]
                if hides:
                    scores = hidden(scores, block * size, places)
                old_max = state[head : head + 1, :]
                new_max = jnp.maximum(old_max, jnp.max(scores, axis=0, keepdims=True))
                weights = jnp.exp(scores - new_max)
                fading = jnp.exp(old_max - new_max)
                state[head : head + 1, :] = new_max
                new_sums.append(sums[head] * fading + jnp.sum(weights, axis=0, keepdims=True))
                here = slice(head * HD, (head + 1) * HD)
                values = kv_turned[head * pair + HD : (head + 1) * pair, at]
                out_total[here, :] = out_total[here, :] * fading + dot(values, weights.astype(low))
            return tuple(new_sums)

        sums = tuple(jnp.zeros((1, TILE), full) for _ in range(heads))
        sums = over_keys(step, by_all, by_some, FORWARD_KEYS, FORWARD_REST, sums)
        for head in range(heads):
            here = slice(head * HD, (head + 1) * HD)
            attended = out_total[here, :] / sums[head]
            log_total = state[head : head + 1, :] + jnp.log(sums[head])
            o_grad = columns_of(o_grad_ref, rows, here).astype(full)
            delta = jnp.sum(o_grad * attended, axis=0, keepdims=True)
            for half, at in enumerate(rows):
                columns = slice(half * RUN, (half + 1) * RUN)
                out_ref[here, at] = attended[:, columns].astype(low)
                log_ref[head : head + 1, at] = log_total[:, columns]
                delta_ref[head : head + 1, at] = delta[:, columns]
        return carry

    lax.fori_loop(0, q_ref.shape[1] // TILE, tile_step, 0)

    block = branch_refs[0].shape[0]
    for piece, ref in enumerate(branch_refs):
        at = slice(piece * block, (piece + 1) * block)
        branch = dot(out_ref[:, at].T, merge_ref[...]) + fed_ref[at, :]
        ref[...] = branch.astype(ref.dtype)


def backward_kernel(
    heads,
    groups,
    runs,
    q_runs_ref,
    q_order_ref,
    k_runs_ref,
    q_ref,
    o_grad_ref,
    kv,
    kv_turned,
    log_ref,
    delta_ref,
    q_grad_ref,
    *refs,
):
    kv_grad_refs = refs[:groups]
    total, first_w, second_w, q_total = refs[groups:]
    pair = 2 * HD
    total[...] = jnp.zeros_like(total)

    def tile_step(tile, carry):
        rows, places, by_all, by_some = tile_of(tile, q_runs_ref, q_order_ref)
        nothing = jnp.zeros((HD, TILE), low)
        for head in range(heads):
            part = slice(head * HD, (head + 1) * HD)
            upper = jnp.concatenate([columns_of(q_ref, rows, part), nothing], axis=0)
            lower = jnp.concatenate([nothing, columns_of(o_grad_ref, rows, part)], axis=0)
            first_w[head, :, :TILE] = upper
            first_w[head, :, TILE:] = lower
            second_w[head, :TILE, :] = upper.T
            second_w[head, TILE:, :] = lower.T
        q_total[...] = jnp.zeros_like(q_total)
        log_totals = columns_of(log_ref, rows)
        deltas = columns_of(delta_ref, rows)

        def step(hides, size, block, carry):
            at = pl.ds(pl.multiple_of(block * size, size), size)
            products = [
                dot(kv[at, head * pair : (head + 1) * pair], first_w[head]) for head in range(heads)
            ]
            for head in range(heads):
                part = slice(head * pair, (head + 1) * pair)
                both = products[head]
                scores = both[:, :TILE]
                if hides:
                    scores = hidden(scores, block * size, places)
                chances = jnp.exp(scores - log_totals[head : head + 1, :])
                score_grad = chances * (both[:, TILE:] - deltas[head : head + 1, :])
                score_grad = score_grad.astype(low)
                joint = jnp.concatenate([score_grad, chances.astype(low)], axis=1)
                total[at, part] += dot(joint, second_w[head])
                here = slice(head * HD, (head + 1) * HD)
                keys = kv_turned[head * pair : head * pair + HD, at]
                q_total[here, :] += dot(keys, score_grad)
            return carry

        over_keys(step, by_all, by_some, BACKWARD_KEYS, BACKWARD_REST, 0)
        for half, at in enumerate(rows):
            q_grad_ref[:, at] = q_total[:, half * RUN : (half + 1) * RUN]
        return carry

    lax.fori_loop(0, q_ref.shape[1] // TILE, tile_step, 0)

    for source in range(groups):

        def give(run, carry, source=source):
            at = pl.multiple_of(k_runs_ref[source * runs + run] * RUN, RUN)
            columns = pl.ds(pl.multiple_of(run * RUN, RUN), RUN)
            rows = total[pl.ds(at, RUN), :].astype(low)
            for head in range(heads):
                part = slice(head * pair, (head + 1) * pair)
                kv_grad_refs[source][part, columns] = rows[:, part].T
            return carry

        lax.fori_loop(0, runs, give, 0)


def attention_call(kernel, name, tables, operands, out_shape, scratch, groups, work):
    width, count = operands[0].shape
    heads, runs = width // HD, count // RUN
    pairs = count * groups * count * heads // 2
    smem = pl.BlockSpec(memory_space=pltpu.SMEM)
    vmem = pl.BlockSpec(memory_space=pltpu.VMEM)
    return pl.pallas_call(
        functools.partial(kernel, heads, groups, runs),
        out_shape=out_shape,
        in_specs=[smem] * len(tables) + [vmem] * len(operands),
        out_specs=tuple([vmem] * len(out_shape)),
        scratch_shapes=scratch,
        compiler_params=pltpu.CompilerParams(vmem_limit_bytes=VMEM),
        cost_estimate=pl.CostEstimate(
            flops=work * pairs,
            bytes_accessed=8 * count * width * groups,
            transcendentals=pairs,
        ),
        name=name,
    )(*tables, *operands)


def pieces_of(block, width):
    kept = jax.ShapeDtypeStruct((block, width), full)
    return (kept,) + (jax.ShapeDtypeStruct((block, width), low),) * (TP - 1)


def attend(tables, queries, o_grads, merge_matrix, fed, kv_parts):
    width, count = queries.shape
    keys = len(kv_parts) * count
    out_shape = (
        jax.ShapeDtypeStruct((width, count), low),
        jax.ShapeDtypeStruct((keys, 2 * width), low),
        jax.ShapeDtypeStruct((2 * width, keys), low),
        jax.ShapeDtypeStruct((8, count), full),
        jax.ShapeDtypeStruct((8, count), full),
    ) + pieces_of(count // TP, fed.shape[1])
    scratch = [
        pltpu.VMEM((width // HD, 2 * HD, TILE), low),
        pltpu.VMEM((8, TILE), full),
        pltpu.VMEM((width, TILE), full),
    ]
    operands = (queries, o_grads, merge_matrix, fed) + tuple(kv_parts)
    groups = len(kv_parts)
    return attention_call(
        forward_kernel, "attend", tables, operands, out_shape, scratch, groups, 6000
    )


def attend_back(tables, queries, o_grads, kv, kv_turned, log_totals, deltas):
    width, count = queries.shape
    keys = kv.shape[0]
    groups = keys // count
    out_shape = (jax.ShapeDtypeStruct((width, count), full),) + (
        jax.ShapeDtypeStruct((2 * width, count), low),
    ) * groups
    scratch = [
        pltpu.VMEM((keys, 2 * width), full),
        pltpu.VMEM((width // HD, 2 * HD, 2 * TILE), low),
        pltpu.VMEM((width // HD, 2 * TILE, 2 * HD), low),
        pltpu.VMEM((width, TILE), full),
    ]
    operands = (queries, o_grads, kv, kv_turned, log_totals, deltas)
    out = attention_call(
        backward_kernel, "attend_back", tables, operands, out_shape, scratch, groups, 6000
    )
    return out[0], out[1:]


def prepare_kernel(heads, order_ref, source_ref, cosine_ref, sine_ref, *refs):
    x_refs, piece_refs, outs = refs[:TP], refs[TP:-6], refs[-6:]
    q_ref, kv_ref, first_ref, second_ref, matrix_ref, small_ref = outs
    span = heads * HD
    block, width = x_refs[0].shape
    rows = jnp.concatenate([piece[...] for piece in piece_refs], axis=0)
    columns = dot(order_ref[...], rows).astype(low)
    turned_columns = columns.T
    matrix = turned_columns[: 3 * span]
    small = turned_columns[3 * span :].astype(full)
    matrix_ref[...] = matrix
    small_ref[...] = small
    gain_one, shift_one, gain_two, shift_two = (small[k : k + 1] for k in range(4))

    shift = jnp.zeros((3 * span, 1), full)
    lane = lax.broadcasted_iota(jnp.int32, (3 * span, HD), 1)
    feature = lax.broadcasted_iota(jnp.int32, (3 * span, width), 1)
    for k in range(3):
        chosen = (source_ref[...] == 3 * feature + k).astype(full).astype(low)
        found = dot(chosen, columns[:, 3 * span :])
        shift += jnp.sum(jnp.where(lane == 6 + k, found, 0.0), axis=1, keepdims=True)

    cosines, sines = cosine_ref[...], sine_ref[...]
    half_dims = ROT // 2

    def rotated(head, at):
        cosine, sine = cosines[:, at], sines[:, at]
        first, second = head[:half_dims], head[half_dims:ROT]
        return jnp.concatenate(
            [first * cosine - second * sine, second * cosine + first * sine, head[ROT:]], axis=0
        )

    for piece in range(TP):
        at = slice(piece * block, (piece + 1) * block)
        x = x_refs[piece][...].astype(full)
        centred = x - jnp.mean(x, axis=1, keepdims=True)
        spread = jnp.mean(centred * centred, axis=1, keepdims=True)
        normed = centred * lax.rsqrt(spread + norm_eps)
        first_low = (normed * gain_one + shift_one).astype(low)
        first_ref[at, :] = first_low
        second_ref[at, :] = (normed * gain_two + shift_two).astype(low)
        joined = dot(matrix, first_low, ((1,), (1,))) + shift
        for head in range(heads):
            here = slice(head * HD, (head + 1) * HD)
            queries = rotated(joined[here], at).astype(low)
            q_ref[here, at] = queries * jnp.asarray(HD**-0.5, low)
            to_key = span + 2 * head * HD
            to_value = to_key + HD
            kv_ref[2 * head * HD : (2 * head + 1) * HD, at] = rotated(
                joined[to_key:to_value], at
            ).astype(low)
            kv_ref[(2 * head + 1) * HD : (2 * head + 2) * HD, at] = joined[
                to_value : to_value + HD
            ].astype(low)


def prepare(heads, order, source, cosines, sines, x_pieces, row_pieces):
    block, width = x_pieces[0].shape
    count, span = TP * block, heads * HD
    return pl.pallas_call(
        functools.partial(prepare_kernel, heads),
        out_shape=(
            jax.ShapeDtypeStruct((span, count), low),
            jax.ShapeDtypeStruct((2 * span, count), low),
            jax.ShapeDtypeStruct((count, width), low),
            jax.ShapeDtypeStruct((count, width), low),
            jax.ShapeDtypeStruct((3 * span, width), low),
            jax.ShapeDtypeStruct((HD, width), full),
        ),
        compiler_params=pltpu.CompilerParams(vmem_limit_bytes=VMEM),
        cost_estimate=pl.CostEstimate(
            flops=50 * width * span * count, bytes_accessed=16 * count * width, transcendentals=count
        ),
        name="prepare",
    )(order, source, cosines, sines, *x_pieces, *row_pieces)


def feed_kernel(
    heads,
    part_ref,
    order_ref,
    back_order_ref,
    unit_order_ref,
    unit_back_order_ref,
    gain_ref,
    shift_ref,
    second_ref,
    *refs,
):
    x_refs, up_refs, piece_refs, refs = refs[:TP], refs[TP : 2 * TP], refs[2 * TP : -11], refs[-11:]
    o_grad_ref, merge_ref, fed_ref, slope_ref, sums_ref, kept_ref, sent_ref = refs[:7]
    expand, reduce, active, gradient = refs[7:]
    span = heads * HD
    block, width = x_refs[0].shape
    units = expand.shape[1]
    rows = jnp.concatenate([piece[...] for piece in piece_refs], axis=0)
    expand[...] = dot(order_ref[...], rows[:, :units]).astype(low)
    reduce[...] = dot(unit_order_ref[...], rows[:, units + width :]).astype(low)
    mine = pl.ds(pl.multiple_of(part_ref[0] * span, span), span)
    merge_ref[...] = dot(order_ref[mine, :], rows[:, units : units + width]).astype(low)
    sums = [jnp.zeros((1, width), full)] * 2 + [jnp.zeros((1, units), full)]
    for piece in range(TP):
        at = slice(piece * block, (piece + 1) * block)
        up = up_refs[piece][...]
        expanded = dot(second_ref[at, :], expand[...]) + shift_ref[...]
        normal = 0.5 + 0.5 * lax.erf(expanded * 0.5**0.5)
        active_low = (expanded * normal).astype(low)
        active[at, :] = active_low
        fed_ref[at, :] = dot(active_low, reduce[...])
        o_grad_ref[:, at] = dot(merge_ref[...], up, ((1,), (1,))).astype(low)
        density = jnp.exp(-0.5 * expanded * expanded) * (2 * math.pi) ** -0.5
        expanded_gradient = dot(up, reduce[...], ((1,), (1,))) * (normal + expanded * density)
        gradient_low = expanded_gradient.astype(low)
        gradient[at, :] = gradient_low
        sums[2] += jnp.sum(gradient_low.astype(full), axis=0, keepdims=True)
        second_gradient = dot(gradient_low, expand[...], ((1,), (1,)))
        x = x_refs[piece][...].astype(full)
        centred = x - jnp.mean(x, axis=1, keepdims=True)
        spread = jnp.mean(centred * centred, axis=1, keepdims=True)
        normed = centred * lax.rsqrt(spread + norm_eps)
        sums[0] += jnp.sum(second_gradient * normed, axis=0, keepdims=True)
        sums[1] += jnp.sum(second_gradient, axis=0, keepdims=True)
        slope_ref[at, :] = second_gradient * gain_ref[...]
    sums_ref[...] = jnp.concatenate(sums + [jnp.zeros((5, width), full)], axis=0)
    up = jnp.concatenate([ref[...] for ref in up_refs], axis=0)
    expand_rows = dot(second_ref[...].T, gradient[...]).astype(low)
    reduce_rows = dot(active[...].T, up).astype(low)
    expand_rows = dot(back_order_ref[...], expand_rows).astype(low)
    reduce_rows = dot(unit_back_order_ref[...], reduce_rows).astype(low)
    half = width // 2
    for ref, at in ((kept_ref, slice(half)), (sent_ref, slice(half, width))):
        ref[:, :units] = expand_rows[at]
        ref[:, units:] = reduce_rows[at]


def feed(heads, part, orders, gain, shift, second_low, x_pieces, up_pieces, row_pieces):
    block, width = x_pieces[0].shape
    count, span, units = TP * block, heads * HD, shift.shape[1]
    rows_shape = jax.ShapeDtypeStruct((width // 2, units + width), low)
    operands = (*orders, gain, shift, second_low, *x_pieces, *up_pieces, *row_pieces)
    vmem = pl.BlockSpec(memory_space=pltpu.VMEM)
    return pl.pallas_call(
        functools.partial(feed_kernel, heads),
        out_shape=(
            jax.ShapeDtypeStruct((span, count), low),
            jax.ShapeDtypeStruct((span, width), low),
            jax.ShapeDtypeStruct((count, width), full),
            jax.ShapeDtypeStruct((count, width), full),
            jax.ShapeDtypeStruct((8, width), full),
            rows_shape,
            rows_shape,
        ),
        in_specs=[pl.BlockSpec(memory_space=pltpu.SMEM)] + [vmem] * len(operands),
        out_specs=(vmem,) * 7,
        scratch_shapes=[
            pltpu.VMEM((width, units), low),
            pltpu.VMEM((units, width), low),
            pltpu.VMEM((count, units), low),
            pltpu.VMEM((count, units), low),
        ],
        compiler_params=pltpu.CompilerParams(vmem_limit_bytes=VMEM),
        cost_estimate=pl.CostEstimate(flops=0, bytes_accessed=0, transcendentals=0),
        name="feed",
    )(part, *operands)


def finish_kernel(
    heads,
    part_ref,
    order_ref,
    place_ref,
    source_ref,
    cosine_ref,
    sine_ref,
    matrix_ref,
    gain_ref,
    early_ref,
    q_grad_ref,
    first_ref,
    slope_in_ref,
    merge_ref,
    *refs,
):
    x_refs, kv_refs, outs = refs[:TP], refs[TP:-5], refs[-5:]
    kept_ref, sent_ref, slope_ref, gradient, joined = outs
    span = heads * HD
    block, width = x_refs[0].shape
    half_dims = ROT // 2
    cosine, sine = cosine_ref[...], sine_ref[...]

    def rotated_back(head):
        first, second = head[:half_dims], head[half_dims:ROT]
        return jnp.concatenate(
            [first * cosine + second * sine, second * cosine - first * sine, head[ROT:]], axis=0
        )

    for head in range(heads):
        here = slice(head * HD, (head + 1) * HD)
        joined[here, :] = rotated_back(q_grad_ref[here, :] * HD**-0.5).astype(low)
        key = slice(2 * head * HD, (2 * head + 1) * HD)
        value = slice((2 * head + 1) * HD, (2 * head + 2) * HD)
        key_grad, value_grad = (
            functools.reduce(jnp.add, [ref[part, :].astype(full) for ref in kv_refs])
            for part in (key, value)
        )
        to_key = span + 2 * head * HD
        joined[to_key : to_key + HD, :] = rotated_back(key_grad).astype(low)
        joined[to_key + HD : to_key + 2 * HD, :] = value_grad.astype(low)

    gain_sum, shift_sum = jnp.zeros((1, width), full), jnp.zeros((1, width), full)
    gain = gain_ref[...]
    for piece in range(TP):
        at = slice(piece * block, (piece + 1) * block)
        x = x_refs[piece][...].astype(full)
        centred = x - jnp.mean(x, axis=1, keepdims=True)
        spread = jnp.mean(centred * centred, axis=1, keepdims=True)
        normed = centred * lax.rsqrt(spread + norm_eps)
        first_gradient = dot(joined[:, at].T, matrix_ref[...])
        gain_sum += jnp.sum(first_gradient * normed, axis=0, keepdims=True)
        shift_sum += jnp.sum(first_gradient, axis=0, keepdims=True)
        slope = first_gradient * gain + slope_in_ref[at, :]
        slope_ref[part_ref[0] ^ piece] = slope.astype(low)

    gradient[...] = dot(joined[...], first_ref[...]).astype(low)
    order = order_ref[...]
    joined_rows = dot(order, gradient[...], ((1,), (1,))).astype(low)
    sums = jnp.concatenate(
        [gain_sum, shift_sum, early_ref[2:, :], jnp.zeros((HD - early_ref.shape[0], width), full)],
        axis=0,
    )
    sums = dot(order, sums.astype(low), ((1,), (1,)))
    joined_sum = jnp.sum(joined[...].astype(full), axis=1, keepdims=True)
    joined_sum = jnp.broadcast_to(joined_sum, (3 * span, HD)).astype(low)
    lane = lax.broadcasted_iota(jnp.int32, (width, HD), 1)
    for k in range(3):
        chosen = (source_ref[...] == 3 * place_ref[...] + k).astype(full).astype(low)
        sums = jnp.where(lane == 5 + k, dot(chosen, joined_sum), sums)
    half = width // 2
    for ref, at in ((kept_ref, slice(half)), (sent_ref, slice(half, width))):
        ref[:, : 3 * span] = joined_rows[at]
        ref[:, 3 * span : 3 * span + HD] = sums[at].astype(low)
        ref[:, 3 * span + HD :] = merge_ref[at, :]


def finish(
    heads,
    part,
    order,
    place,
    source,
    cosines,
    sines,
    matrix,
    gain,
    early,
    q_grad,
    first_low,
    slope,
    merge_rows,
    x_pieces,
    kv_grads,
):
    block, width = x_pieces[0].shape
    count, span = TP * block, heads * HD
    return pl.pallas_call(
        functools.partial(finish_kernel, heads),
        out_shape=(
            jax.ShapeDtypeStruct((width // 2, 3 * span + HD + width), low),
            jax.ShapeDtypeStruct((width // 2, 3 * span + HD + width), low),
            jax.ShapeDtypeStruct((TP, block, width), low),
        ),
        in_specs=[pl.BlockSpec(memory_space=pltpu.SMEM)]
        + [pl.BlockSpec(memory_space=pltpu.VMEM)] * (12 + TP + len(kv_grads)),
        scratch_shapes=[pltpu.VMEM((3 * span, width), low), pltpu.VMEM((3 * span, count), low)],
        compiler_params=pltpu.CompilerParams(vmem_limit_bytes=VMEM),
        cost_estimate=pl.CostEstimate(
            flops=50 * width * span * count, bytes_accessed=16 * count * width, transcendentals=count
        ),
        name="finish",
    )(
        part,
        order,
        place,
        source,
        cosines,
        sines,
        matrix,
        gain,
        early,
        q_grad,
        first_low,
        slope,
        merge_rows,
        *x_pieces,
        *kv_grads,
    )


def tokens_kernel(x_ref, cotangent_ref, slopes_ref, out_ref):
    x = x_ref[...].astype(full)
    centred = x - jnp.mean(x, axis=1, keepdims=True)
    inverse = lax.rsqrt(jnp.mean(centred * centred, axis=1, keepdims=True) + norm_eps)
    normed = centred * inverse
    slope = functools.reduce(jnp.add, [slopes_ref[part].astype(full) for part in range(TP)])
    slope_mean = jnp.mean(slope, axis=1, keepdims=True)
    along = jnp.mean(slope * normed, axis=1, keepdims=True)
    out_ref[...] = cotangent_ref[...].astype(full) + inverse * (slope - slope_mean - normed * along)


def tokens_gradient(x_low, cotangent, slopes):
    return pl.pallas_call(
        tokens_kernel,
        out_shape=jax.ShapeDtypeStruct(x_low.shape, full),
        compiler_params=pltpu.CompilerParams(vmem_limit_bytes=VMEM),
        name="tokens_gradient",
    )(x_low, cotangent, slopes)


def on_device(
    tokens,
    positions,
    gain_attention,
    bias_attention,
    gain_feed,
    bias_feed,
    weight_joined,
    bias_joined,
    weight_merge,
    bias_merge,
    weight_expand,
    bias_expand,
    weight_reduce,
    bias_reduce,
    cotangent,
):
    seqs, block, width = tokens.shape
    units = weight_expand.shape[1]
    copies = lax.axis_size("dp")
    members = lax.axis_size("blk")
    groups = members // TP
    here = lax.axis_index("blk")
    my_part, my_group, my_copy = here // groups, here % groups, lax.axis_index("dp")
    heads = width // HD // TP
    depth = weight_joined.shape[0]
    part_units = units // TP
    my_units = weight_reduce.shape[0]
    span = heads * HD

    def over_parts(value, away):
        return lax.ppermute(value, "blk", [(i, i ^ (away * groups)) for i in range(members)])

    def over_groups(value, away):
        return lax.ppermute(value, "blk", [(i, i ^ away) for i in range(members)])

    def over_copies(value, away):
        return lax.ppermute(value, "dp", [(i, i ^ away) for i in range(copies)])

    part_lines = [[part * groups + g for part in range(TP)] for g in range(groups)]
    group_planes = [[part * groups + g for g in range(groups)] for part in range(TP)]

    def swapped(value, lines):
        return lax.all_to_all(value, "blk", 0, 0, axis_index_groups=lines, tiled=True)

    def from_mine(value, me, axis):
        count = value.shape[axis]
        bit = 1
        while bit < count:
            split = value.reshape(value.shape[:axis] + (-1, 2, bit) + value.shape[axis + 1 :])
            flipped = jnp.flip(split, axis + 1).reshape(value.shape)
            value = jnp.where(me // bit % 2 == 1, flipped, value)
            bit *= 2
        return value

    def picked(value, at, axis):
        return lax.dynamic_index_in_dim(value, at, axis, keepdims=False)

    def exchanged(value, move, count, me, axis):
        return [picked(value, me, axis)] + [
            move(picked(value, me ^ away, axis), away) for away in range(1, count)
        ]

    def halved(value, move, count, me):
        while count > 1:
            count //= 2
            halves = value.reshape((2, count) + value.shape[1:])
            upper = me // count % 2
            sent = move(picked(halves, 1 - upper, 0).astype(low), count)
            value = picked(halves, upper, 0).astype(full) + sent.astype(full)
        return value[0]

    def ready(value):
        first = value[(0,) * value.ndim]
        return first == first

    def added(pieces):
        return functools.reduce(jnp.add, [piece.astype(full) for piece in pieces])

    def placed(pieces, me):
        out = jnp.zeros((len(pieces),) + pieces[0].shape, pieces[0].dtype)
        for away, piece in enumerate(pieces):
            out = lax.dynamic_update_index_in_dim(out, piece, me ^ away, 0)
        return out

    def of_group(value):
        return jnp.concatenate([value] + [over_parts(value, away) for away in range(1, TP)], axis=0)

    count = TP * block
    runs = count // RUN

    def as_columns(vector):
        return vector.reshape(depth, -1)

    starts = (positions.reshape(-1)[::RUN] // RUN).astype(low)
    starts = jnp.pad(starts, (0, depth - starts.shape[0]))
    small = jnp.concatenate(
        [
            as_columns(vector)
            for vector in (
                gain_attention,
                bias_attention,
                gain_feed,
                bias_feed,
                bias_merge,
                bias_reduce,
                bias_joined,
                bias_expand,
                starts,
            )
        ],
        axis=1,
    )
    small = jnp.pad(small, ((0, 0), (0, HD - small.shape[1])))

    def by_head(matrix):
        lead = matrix.shape[:-1]
        split = matrix.reshape(lead + (3, TP, heads, HD))
        queries = split[..., 0, :, :, :].reshape(lead + (TP, span))
        kv = jnp.stack([split[..., 1, :, :, :], split[..., 2, :, :, :]], axis=-2)
        return jnp.concatenate([queries, kv.reshape(lead + (TP, 2 * span))], axis=-1)

    def from_head(matrix):
        lead = matrix.shape[:-2]
        queries = matrix[..., :span].reshape(lead + (1, TP, heads, HD))
        kv = matrix[..., span:].reshape(lead + (TP, heads, 2, HD))
        kv = jnp.moveaxis(kv, -2, len(lead))
        return jnp.concatenate([queries, kv], axis=len(lead)).reshape(lead + (3 * width,))

    expand_parts = weight_expand.reshape(depth, copies, TP, groups * my_units)
    expand_parts = jnp.moveaxis(expand_parts, 2, 0).reshape(TP, depth, part_units)
    parts = jnp.concatenate(
        [
            expand_parts,
            jnp.broadcast_to(weight_merge, (TP, depth, width)),
            jnp.swapaxes(by_head(weight_joined), 0, 1),
            jnp.broadcast_to(small, (TP, depth, HD)),
        ],
        axis=2,
    )
    tokens = jnp.where(ready(parts), tokens, jnp.zeros_like(tokens))
    to_merge, to_joined = part_units, part_units + width
    to_small = 3 * span
    mine = swapped(parts, part_lines).reshape(my_units, -1)
    own_low = tokens.reshape(block, width)
    own_later, _ = lax.optimization_barrier((own_low, mine))
    x_pieces = [own_low, over_parts(own_low, 1)]
    x_pieces += [over_parts(own_later, away) for away in range(2, TP)]
    rows = own_low.astype(full)
    first_rows = mine[:, to_joined:]
    mine = jnp.concatenate([mine[:, :to_joined], weight_reduce], axis=1)
    def in_plane(value):
        value = swapped(jnp.broadcast_to(value, (groups,) + value.shape), group_planes)
        return value.reshape(groups * my_units, -1)

    def of_copies(value):
        return [value] + [over_copies(value, away) for away in range(1, copies)]

    near = in_plane(first_rows)
    row_pieces = of_copies(near)
    rest_pieces = of_copies(in_plane(mine))
    up_low, *_ = lax.optimization_barrier((cotangent, *x_pieces[1:]))
    up_low = up_low.reshape(block, width)
    up_pieces = [up_low] + [over_parts(up_low, away) for away in range(1, TP)]
    came = jnp.arange(width, dtype=jnp.int32)
    row, came_part = came % depth, (came // depth) % TP
    came_group = (came // (depth * TP)) % groups
    came_copy = came // (depth * TP * groups) ^ my_copy
    place_of = ((came_copy * TP + came_part) * groups + came_group) * depth + row
    wanted = jnp.arange(width, dtype=jnp.int32)[:, None]
    order = (place_of[None, :] == wanted).astype(low)
    back_order = (place_of[:, None] == wanted[:, 0]).astype(low)
    source = jnp.arange(3 * width, dtype=jnp.int32)
    unit = jnp.arange(part_units, dtype=jnp.int32)
    unit_group = (unit // my_units) % groups
    unit_copy = unit // (my_units * groups) ^ my_copy
    unit_place = (unit_copy * groups + unit_group) * my_units + unit % my_units
    unit_order = (unit_place[None, :] == unit[:, None]).astype(low)

    unit_back_order = (unit_place[:, None] == unit[None, :]).astype(low)
    head_order = lax.dynamic_slice_in_dim(order, my_part * span, span, 0)

    run_starts = near[:, to_small + 13].reshape(groups, TP, depth)
    run_starts = from_mine(from_mine(run_starts, my_group, 0), my_part, 1)
    k_runs = run_starts[:, :, : block // RUN].astype(jnp.int32).reshape(groups, runs)
    q_runs = k_runs[0]
    places = (q_runs[:, None] * RUN + jnp.arange(RUN, dtype=jnp.int32)).reshape(count)

    half_dims = ROT // 2
    frequency = jnp.exp(jnp.arange(half_dims, dtype=full) * (-2.0 * math.log(10000.0) / ROT))
    angles = frequency[:, None] * places.astype(full)
    cosines, sines = jnp.cos(angles), jnp.sin(angles)
    my_source = picked(by_head(source), my_part, 0)
    queries, kv, first_low, second_low, joined_matrix, small_all = prepare(
        heads, order, my_source[:, None], cosines, sines, x_pieces, row_pieces
    )
    gain_one, _, gain_two, _, merge_shift, reduce_shift = small_all[:6]
    expand_shift = jnp.swapaxes(small_all[9:13], 0, 1)
    expand_shift = picked(expand_shift.reshape(copies, TP, groups * my_units), my_part, 1)
    expand_shift = expand_shift.reshape(-1)
    rank = jnp.sum(q_runs[None, :] < q_runs[:, None], axis=1)
    index = jnp.arange(runs, dtype=jnp.int32)
    q_order = jnp.sum(jnp.where(rank[None, :] == index[:, None], index[None, :], 0), axis=1)
    kv_parts = [kv] + [over_groups(kv, away) for away in range(1, groups)]

    tables = (q_runs, q_order.astype(jnp.int32), k_runs.reshape(-1))
    def sent_halves(value, move, count):
        while count > 1:
            count //= 2
            value = value.reshape((2, -1) + value.shape[1:])
            value = value[0].astype(full) + move(value[1].astype(low), count).astype(full)
        return value

    def over_copies_halved(kept, sent):
        value = kept.astype(full) + over_copies(sent, copies // 2).astype(full)
        return sent_halves(value, over_copies, copies // 2).astype(low)

    def over_plane(value):
        return swapped(value.reshape(groups, my_units, -1), group_planes)

    attended_gradient, merge_matrix, fed, second_slope, feed_sums, *later = feed(
        heads,
        my_part[None].astype(jnp.int32),
        (order, back_order, unit_order, unit_back_order),
        gain_two[None, :],
        expand_shift[None, :],
        second_low,
        x_pieces,
        up_pieces,
        rest_pieces,
    )
    kv_parts, later = lax.optimization_barrier((kv_parts, later))
    later = over_plane(over_copies_halved(*later))

    attended_low, kv_sorted, kv_turned, log_totals, deltas, *branches = attend(
        tables, queries, attended_gradient, merge_matrix, fed, kv_parts
    )
    log_totals, later = lax.optimization_barrier((log_totals, later))
    query_total, kv_totals = attend_back(
        tables, queries, attended_gradient, kv_sorted, kv_turned, log_totals, deltas
    )

    def of_rows(pieces):
        return [pieces[0]] + [over_parts(pieces[away], away) for away in range(1, TP)]

    branches, _ = lax.optimization_barrier((of_rows(branches), query_total))
    branches = added(branches)
    result = (rows + branches + merge_shift + reduce_shift).astype(low)

    attended_then, kv_totals, _, _ = lax.optimization_barrier(
        (attended_low, kv_totals, query_total, result)
    )
    later = jnp.sum(later.astype(full), axis=0)
    gradient_weight_reduce = later[:, part_units:]
    merge_rows = dot(attended_then, jnp.concatenate(up_pieces, axis=0)).astype(low)
    merge_rows = dot(head_order, merge_rows, ((0,), (0,))).astype(low)
    later = later[:, :part_units].astype(low)

    upstream = cotangent.reshape(block, width).astype(full)
    expand_sum = feed_sums[2].reshape(copies, -1)
    expand_sum = jnp.swapaxes(placed_alone(expand_sum, my_part, TP), 0, 1).reshape(width, -1)
    nothing = jnp.zeros((width,), full)
    early = [nothing, nothing, feed_sums[0], feed_sums[1], jnp.sum(upstream, axis=0)]
    early = jnp.stack(early + [nothing] * 3)
    early = jnp.concatenate([early, expand_sum.T], axis=0)
    kv_grads = [kv_totals[0]] + [over_groups(kv_totals[r], r) for r in range(1, groups)]
    final_kept, final_sent, slopes = finish(
        heads,
        my_part[None].astype(jnp.int32),
        back_order,
        place_of[:, None],
        my_source[None, :],
        cosines,
        sines,
        joined_matrix,
        gain_one[None, :],
        early,
        query_total,
        first_low,
        second_slope,
        merge_rows,
        x_pieces,
        kv_grads,
    )
    slopes = swapped(slopes, part_lines)
    gradient_tokens = tokens_gradient(own_low, cotangent.reshape(block, width), slopes)

    final = over_copies_halved(final_kept, final_sent).reshape(groups, my_units, -1)
    final = added(exchanged(final, over_groups, groups, my_group, 0)).astype(low)
    final, _ = lax.optimization_barrier((final, slopes))
    final = jnp.concatenate([final, later], axis=1).reshape(TP, depth, -1)
    final = placed(exchanged(final, over_parts, TP, my_part, 0), my_part)
    to_rest = 3 * span + HD
    gradient_weight_joined = from_head(jnp.swapaxes(final[..., : 3 * span], 0, 1))
    small_total = jnp.sum(final[..., 3 * span : to_rest].astype(full), axis=0)
    gradient_weight_merge = jnp.sum(final[..., to_rest : to_rest + width].astype(full), axis=0)
    gradient_weight_expand = final[..., to_rest + width :]
    gradient_weight_expand = jnp.moveaxis(
        gradient_weight_expand.reshape(TP, depth, copies, groups * my_units), 0, 2
    ).reshape(depth, units)
    gradients = small_total[:, :5].T
    gradient_bias_joined = small_total[:, 5:8].reshape(-1)
    gradient_bias_expand = small_total[:, 8:12].reshape(-1)

    def wide(value):
        return value.astype(full)

    return (
        result.reshape(tokens.shape),
        gradient_tokens.reshape(tokens.shape),
        gradients[0],
        gradients[1],
        gradients[2],
        gradients[3],
        wide(gradient_weight_joined),
        gradient_bias_joined,
        wide(gradient_weight_merge),
        gradients[4],
        wide(gradient_weight_expand),
        gradient_bias_expand,
        wide(gradient_weight_reduce),
        gradients[4],
    )


def placed_alone(value, at, count):
    out = jnp.zeros((count,) + value.shape, value.dtype)
    return lax.dynamic_update_index_in_dim(out, value, at, 0)


def solution(mesh):
    rows = P("dp", "blk", None)
    vector, matrix = P(("dp", "blk")), P(("dp", "blk"), None)
    params = (vector,) * 4 + (matrix, vector) * 4
    return jax.shard_map(
        on_device,
        mesh=mesh,
        in_specs=(rows, P("dp", "blk")) + params + (rows,),
        out_specs=(rows, rows) + params,
        check_vma=False,
    )
```

profile of v0, /device:TPU:0, one launch (start us, length us, event | category | flops | bytes accessed | tf_op | source)
XLA Modules:
  0.0 307.2 jit_solution(12561539853309147985)
XLA Ops:
  5.3 6.3 %all-to-all-start = ((bf16[4,24,2176]{2,1,0:T(8,128)(2,1)}), bf16[4,24,2176]{2,1,0:T(8,128)(2,1)S(1)}, u32[]{:S(2)}, u32[]{:S(2)}) async-start(bf16[4,24,2176]{2,1,0:T(8,128)(2,1)} %concatenate.29), calls=%async_computation | async-start | bytes 835584 | tf_op jit(solution)/shard_map/all_to_all | solution.py:639
  15.9 2.4 iota_compare_fusion.3
  18.3 5.4 %all-to-all-done = bf16[4,24,2176]{2,1,0:T(8,128)(2,1)S(1)} async-done(((bf16[4,24,2176]{2,1,0:T(8,128)(2,1)}), bf16[4,24,2176]{2,1,0:T(8,128)(2,1)S(1)}, u32[]{:S(2)}, u32[]{:S(2)}) %all-to-all-start) | async-done | bytes 417824 | tf_op jit(solution)/shard_map/all_to_all | solution.py:639
  24.5 3.7 %all-to-all-start.1 = ((bf16[4,96,640]{2,1,0:T(8,128)(2,1)}), bf16[4,96,640]{2,1,0:T(8,128)(2,1)S(1)}, u32[]{:S(2)}, u32[]{:S(2)}) async-start(bf16[4,96,640]{2,1,0:T(8,128)(2,1)} %broadcast_in_dim.73), calls=%async_computation.1 | async-start | bytes 983040 | tf_op jit(solution)/shard_map/all_to_all | solution.py:639
  29.3 3.2 %collective-permute-start.2 = (bf16[256,768]{1,0:T(8,128)(2,1)S(1)}, bf16[256,768]{1,0:T(8,128)(2,1)}, u32[]{:S(2)}, u32[]{:S(2)}) collective-permute-start(bf16[256,768]{1,0:T(8,128)(2,1)S(1)} %select_bitcast_fusion.refs_0_.x_ref), channel_id=1, source_target_pairs={{0,12},{1,13},{2,14},{3,15},{4,8},{5,9},{6,10},{7,11},{8,4},{9,5},... | collective-permute-start | bytes 1179656 | tf_op jit(solution)/shard_map/ppermute | solution.py:627
  36.0 3.9 %all-to-all-start.2 = ((bf16[4,96,2304]{2,1,0:T(8,128)(2,1)}), bf16[4,96,2304]{2,1,0:T(8,128)(2,1)S(1)}, u32[]{:S(2)}, u32[]{:S(2)}) async-start(bf16[4,96,2304]{2,1,0:T(8,128)(2,1)} %broadcast_in_dim.78), calls=%async_computation.2 | async-start | bytes 3538944 | tf_op jit(solution)/shard_map/all_to_all | solution.py:639
  41.0 17.2 %all-to-all-done.2 = bf16[4,96,2304]{2,1,0:T(8,128)(2,1)S(1)} async-done(((bf16[4,96,2304]{2,1,0:T(8,128)(2,1)}), bf16[4,96,2304]{2,1,0:T(8,128)(2,1)S(1)}, u32[]{:S(2)}, u32[]{:S(2)}) %all-to-all-start.2) | async-done | bytes 1769504 | tf_op jit(solution)/shard_map/all_to_all | solution.py:639
  59.3 5.5 %collective-permute-start.4 = (bf16[256,768]{1,0:T(8,128)(2,1)S(1)}, bf16[256,768]{1,0:T(8,128)(2,1)S(1)}, u32[]{:S(2)}, u32[]{:S(2)}) collective-permute-start(bf16[256,768]{1,0:T(8,128)(2,1)S(1)} %bitcast.106), channel_id=1, source_target_pairs={{0,4},{1,5},{2,6},{3,7},{4,0},{5,1},{6,2},{7,3},{8,12},{9,13},{10,... | collective-permute-start | bytes 1179656 | tf_op jit(solution)/shard_map/ppermute | solution.py:627
  64.8 7.9 %prepare.1 = (bf16[192,1024]{1,0:T(8,128)(2,1)}, bf16[384,1024]{1,0:T(8,128)(2,1)}, bf16[1024,768]{1,0:T(8,128)(2,1)}, bf16[1024,768]{1,0:T(8,128)(2,1)}, bf16[576,768]{1,0:T(8,128)(2,1)}, /*index=5*/f32[64,768]{1,0:T(8,128)}) custom-call(bf16[768,768]{1,0:T(8,128)(2,1)} %get-tuple-element.139.order_ref, s32[576,1]{1,0:T(8,128)} %copy.86.source_ref, ...), custom_call_target="tpu_custom_call" | custom-call | flops 7549747200 | bytes 12582912 | tf_op jit(solution)/shard_map/prepare/pallas_call | solution.py:337
  72.7 2.6 collective-permute-start.10
  75.8 5.5 %collective-permute-done.4.refs_5_ = bf16[256,768]{1,0:T(8,128)(2,1)S(1)} collective-permute-done((bf16[256,768]{1,0:T(8,128)(2,1)S(1)}, bf16[256,768]{1,0:T(8,128)(2,1)S(1)}, u32[]{:S(2)}, u32[]{:S(2)}) %collective-permute-start.4) | collective-permute-done | bytes 393248 | tf_op jit(solution)/shard_map/ppermute | solution.py:627
  89.7 6.5 %collective-permute-done.6.refs_7_ = bf16[256,768]{1,0:T(8,128)(2,1)S(1)} collective-permute-done((bf16[256,768]{1,0:T(8,128)(2,1)S(1)}, bf16[256,768]{1,0:T(8,128)(2,1)S(1)}, u32[]{:S(2)}, u32[]{:S(2)}) %collective-permute-start.6) | collective-permute-done | bytes 393248 | tf_op jit(solution)/shard_map/ppermute | solution.py:627
  97.0 19.1 %feed.1 = (bf16[192,1024]{1,0:T(8,128)(2,1)}, bf16[192,768]{1,0:T(8,128)(2,1)}, f32[1024,768]{1,0:T(8,128)}, f32[1024,768]{1,0:T(8,128)}, f32[8,768]{1,0:T(8,128...) custom-call(s32[1]{0:T(128)} %bitcast.30.part_ref, bf16[768,768]{1,0:T(8,128)(2,1)} %get-tuple-element.139.order_ref, ...), custom_call_target="tpu_custom_call" | custom-call | tf_op jit(solution)/shard_map/feed/pallas_call | solution.py:419
  119.2 2.6 add_convert_fusion
  121.8 3.5 %all-to-all-start.3 = ((bf16[4,96,1536]{2,1,0:T(8,128)(2,1)}), bf16[4,96,1536]{2,1,0:T(8,128)(2,1)S(1)}, u32[]{:S(2)}, u32[]{:S(2)}) async-start(bf16[4,96,1536]{2,1,0:T(8,128)(2,1)} %bitcast.35), calls=%async_computation.3 | async-start | bytes 2359296 | tf_op jit(solution)/shard_map/all_to_all | solution.py:639
  125.3 21.8 %attend.1 = (bf16[192,1024]{1,0:T(8,128)(2,1)}, bf16[4096,384]{1,0:T(8,128)(2,1)}, bf16[384,4096]{1,0:T(8,128)(2,1)}, f32[8,1024]{1,0:T(8,128)}, f32[8,1024]{1,0...) custom-call(s32[8]{0:T(128)} %copy-done.20, ...), custom_call_target="tpu_custom_call" | custom-call | flops 37748736000 | bytes 6291456 | tf_op jit(solution)/shard_map/attend/pallas_call | solution.py:215
  147.1 6.9 %collective-permute-start.11 = (bf16[256,768]{1,0:T(8,128)(2,1)}, bf16[256,768]{1,0:T(8,128)(2,1)S(1)}, u32[]{:S(2)}, u32[]{:S(2)}) collective-permute-start(bf16[256,768]{1,0:T(8,128)(2,1)} %get-tuple-element.80), channel_id=1, source_target_pairs={{0,4},{1,5},{2,6},{3,7},{4,0},{5,1},{6,2},{7,3},{8,12},{9,13},{10,... | collective-permute-start | bytes 1179656 | tf_op jit(solution)/shard_map/ppermute | solution.py:627
  154.2 2.3 collective-permute-start.13
  156.5 27.1 %attend_back.1 = (f32[192,1024]{1,0:T(8,128)}, bf16[384,1024]{1,0:T(8,128)(2,1)}, bf16[384,1024]{1,0:T(8,128)(2,1)}, bf16[384,1024]{1,0:T(8,128)(2,1)}, bf16[384,1024]{1,0:T(8,128)(2,1)}) custom-call(s32[8]{0:T(128)} %copy-done.20, s32[8]{0:T(128)} %select_reduce_fusion.q_order_ref, s32[32]{0:T(128)} %reshape_reshape.3.k_runs_ref, ...), custom_call_target="tpu_custom_call" | custom-call | flops 37748736000 | bytes 6291456 | tf_op jit(solution)/shard_map/attend_back/pallas_call | solution.py:215
  184.1 2.2 add_convert_fusion.2
  186.3 6.7 %collective-permute-start.15 = (bf16[384,1024]{1,0:T(8,128)(2,1)}, bf16[384,1024]{1,0:T(8,128)(2,1)}, u32[]{:S(2)}, u32[]{:S(2)}) collective-permute-start(bf16[384,1024]{1,0:T(8,128)(2,1)} %get-tuple-element.106), channel_id=1, source_target_pairs={{0,1},{1,0},{2,3},{3,2},{4,5},{5,4},{6,7},{7,6},{8,9},{9,8},{10,11... | collective-permute-start | bytes 2359304 | tf_op jit(solution)/shard_map/ppermute | solution.py:630
  193.0 5.5 %collective-permute-start.16 = (bf16[384,1024]{1,0:T(8,128)(2,1)}, bf16[384,1024]{1,0:T(8,128)(2,1)}, u32[]{:S(2)}, u32[]{:S(2)}) collective-permute-start(bf16[384,1024]{1,0:T(8,128)(2,1)} %get-tuple-element.107), channel_id=1, source_target_pairs={{0,2},{1,3},{2,0},{3,1},{4,6},{5,7},{6,4},{7,5},{8,10},{9,11},{10,... | collective-permute-start | bytes 2359304 | tf_op jit(solution)/shard_map/ppermute | solution.py:630
  203.5 3.0 convolution_convert_fusion.merge_ref
  207.8 24.3 %collective-permute-done.16.refs_6_ = bf16[384,1024]{1,0:T(8,128)(2,1)} collective-permute-done((bf16[384,1024]{1,0:T(8,128)(2,1)}, bf16[384,1024]{1,0:T(8,128)(2,1)}, u32[]{:S(2)}, u32[]{:S(2)}) %collective-permute-start.16) | collective-permute-done | bytes 786464 | tf_op jit(solution)/shard_map/ppermute | solution.py:630
  232.1 12.5 %finish.1 = (bf16[384,1408]{1,0:T(8,128)(2,1)}, bf16[384,1408]{1,0:T(8,128)(2,1)}, bf16[4,256,768]{2,1,0:T(8,128)(2,1)}) custom-call(s32[1]{0:T(128)} %bitcast.30.part_ref, bf16[768,768]{1,0:T(8,128)(2,1)} %get-tuple-element.140.back_order_ref.order_ref, s32[768,1]{1,0:T(8,128)} %fusion.32.place_ref, s32[1,576]{1,0:T(1,128)} %copy-done.18, ...), custom_call_target="tpu_custom_call" | custom-call | flops 7549747200 | bytes 12582912 | tf_op jit(solution)/shard_map/finish/pallas_call | solution.py:542
  246.4 4.8 %all-to-all-start.4 = ((bf16[4,256,768]{2,1,0:T(8,128)(2,1)}), bf16[4,256,768]{2,1,0:T(8,128)(2,1)S(1)}, u32[]{:S(2)}, u32[]{:S(2)}) async-start(bf16[4,256,768]{2,1,0:T(8,128)(2,1)} %get-tuple-element.109), calls=%async_computation.4 | async-start | bytes 3145728 | tf_op jit(solution)/shard_map/all_to_all | solution.py:639
  258.6 6.0 %collective-permute-done.19 = bf16[96,1408]{1,0:T(8,128)(2,1)} collective-permute-done((bf16[96,1408]{1,0:T(8,128)(2,1)}, bf16[96,1408]{1,0:T(8,128)(2,1)}, u32[]{:S(2)}, u32[]{:S(2)}) %collective-permute-start.19) | collective-permute-done | bytes 270368 | tf_op jit(solution)/shard_map/ppermute | solution.py:630
  264.6 4.4 %collective-permute-done.20 = bf16[96,1408]{1,0:T(8,128)(2,1)} collective-permute-done((bf16[96,1408]{1,0:T(8,128)(2,1)}, bf16[96,1408]{1,0:T(8,128)(2,1)}, u32[]{:S(2)}, u32[]{:S(2)}) %collective-permute-start.20) | collective-permute-done | bytes 270368 | tf_op jit(solution)/shard_map/ppermute | solution.py:630
  272.1 16.6 %all-to-all-done.4.slopes_ref = bf16[4,256,768]{2,1,0:T(8,128)(2,1)S(1)} async-done(((bf16[4,256,768]{2,1,0:T(8,128)(2,1)}), bf16[4,256,768]{2,1,0:T(8,128)(2,1)S(1)}, u32[]{:S(2)}, u32[]{:S(2)}) %all-to-all-start.4) | async-done | bytes 1572896 | tf_op jit(solution)/shard_map/all_to_all | solution.py:639
  289.9 2.3 collective-permute-start.23
  294.1 3.2 %tokens_gradient.1 = f32[256,768]{1,0:T(8,128)} custom-call(bf16[256,768]{1,0:T(8,128)(2,1)} %copy-done.5, bf16[256,768]{1,0:T(8,128)(2,1)} %bitcast.105, bf16[4,256,768]{2,1,0:T(8,128)(2,1)} %copy-done.1), custom_call_target="tpu_custom_call" | custom-call | tf_op jit(solution)/shard_map/tokens_gradient/pallas_call | solution.py:588
  297.3 3.4 %collective-permute-done.23 = bf16[24,2176]{1,0:T(8,128)(2,1)S(1)} collective-permute-done((bf16[24,2176]{1,0:T(8,128)(2,1)S(1)}, bf16[24,2176]{1,0:T(8,128)(2,1)S(1)}, u32[]{:S(2)}, u32[]{:S(2)}) %collective-permute-start.23) | collective-permute-done | bytes 104480 | tf_op jit(solution)/shard_map/ppermute | solution.py:627
  (217 shorter events, 56.2 us)
Async XLA Ops:
  5.3 18.4 %all-to-all-start = ((bf16[4,24,2176]{2,1,0:T(8,128)(2,1)}), bf16[4,24,2176]{2,1,0:T(8,128)(2,1)S(1)}, u32[]{:S(2)}, u32[]{:S(2)}) async-start(bf16[4,24,2176]{2,1,0:T(8,128)(2,1)} %concatenate.29), calls=%async_computation | async-start | bytes 835584 | tf_op jit(solution)/shard_map/all_to_all | solution.py:639
  13.5 45.8 %collective-permute-start = (bf16[256,768]{1,0:T(8,128)(2,1)S(1)}, bf16[256,768]{1,0:T(8,128)(2,1)}, u32[]{:S(2)}, u32[]{:S(2)}) collective-permute-start(bf16[256,768]{1,0:T(8,128)(2,1)S(1)} %select_bitcast_fusion.refs_0_.x_ref), channel_id=1, source_target_pairs={{0,4},{1,5},{2,6},{3,7},{4,0},{5,1},{6,2},{7,3},{8,12},{9,13},{10,... | collective-permute-start | bytes 1179656 | tf_op jit(solution)/shard_map/ppermute | solution.py:627
  24.5 10.1 %all-to-all-start.1 = ((bf16[4,96,640]{2,1,0:T(8,128)(2,1)}), bf16[4,96,640]{2,1,0:T(8,128)(2,1)S(1)}, u32[]{:S(2)}, u32[]{:S(2)}) async-start(bf16[4,96,640]{2,1,0:T(8,128)(2,1)} %broadcast_in_dim.73), calls=%async_computation.1 | async-start | bytes 983040 | tf_op jit(solution)/shard_map/all_to_all | solution.py:639
  29.3 30.0 %collective-permute-start.1 = (bf16[256,768]{1,0:T(8,128)(2,1)S(1)}, bf16[256,768]{1,0:T(8,128)(2,1)}, u32[]{:S(2)}, u32[]{:S(2)}) collective-permute-start(bf16[256,768]{1,0:T(8,128)(2,1)S(1)} %select_bitcast_fusion.refs_0_.x_ref), channel_id=1, source_target_pairs={{0,8},{1,9},{2,10},{3,11},{4,12},{5,13},{6,14},{7,15},{8,0},{9,1},... | collective-permute-start | bytes 1179656 | tf_op jit(solution)/shard_map/ppermute | solution.py:627
  29.3 30.0 %collective-permute-start.2 = (bf16[256,768]{1,0:T(8,128)(2,1)S(1)}, bf16[256,768]{1,0:T(8,128)(2,1)}, u32[]{:S(2)}, u32[]{:S(2)}) collective-permute-start(bf16[256,768]{1,0:T(8,128)(2,1)S(1)} %select_bitcast_fusion.refs_0_.x_ref), channel_id=1, source_target_pairs={{0,12},{1,13},{2,14},{3,15},{4,8},{5,9},{6,10},{7,11},{8,4},{9,5},... | collective-permute-start | bytes 1179656 | tf_op jit(solution)/shard_map/ppermute | solution.py:627
  36.0 22.2 %all-to-all-start.2 = ((bf16[4,96,2304]{2,1,0:T(8,128)(2,1)}), bf16[4,96,2304]{2,1,0:T(8,128)(2,1)S(1)}, u32[]{:S(2)}, u32[]{:S(2)}) async-start(bf16[4,96,2304]{2,1,0:T(8,128)(2,1)} %broadcast_in_dim.78), calls=%async_computation.2 | async-start | bytes 3538944 | tf_op jit(solution)/shard_map/all_to_all | solution.py:639
  40.6 24.1 %collective-permute-start.3 = (bf16[384,640]{1,0:T(8,128)(2,1)S(1)}, bf16[384,640]{1,0:T(8,128)(2,1)}, u32[]{:S(2)}, u32[]{:S(2)}) collective-permute-start(bf16[384,640]{1,0:T(8,128)(2,1)S(1)} %bitcast.116), channel_id=1, source_target_pairs={{0,16},{16,0},{1,17},{17,1},{2,18},{18,2},{3,19},{19,3},{4,20},{20... | collective-permute-start | bytes 1474568 | tf_op jit(solution)/shard_map/ppermute | solution.py:633
  41.0 75.8 %copy-start.20 = (s32[8]{0:T(128)}, s32[8]{0:T(128)S(1)}, u32[]{:S(2)}) copy-start(s32[8]{0:T(128)S(1)} %squeeze.46.q_runs_ref) | copy-start | bytes 100
  58.2 38.0 %collective-permute-start.7 = (bf16[384,2304]{1,0:T(8,128)(2,1)S(1)}, bf16[384,2304]{1,0:T(8,128)(2,1)}, u32[]{:S(2)}, u32[]{:S(2)}) collective-permute-start(bf16[384,2304]{1,0:T(8,128)(2,1)S(1)} %bitcast.100), channel_id=1, source_target_pairs={{0,16},{16,0},{1,17},{17,1},{2,18},{18,2},{3,19},{19,3},{4,20},{20... | collective-permute-start | bytes 5308424 | tf_op jit(solution)/shard_map/ppermute | solution.py:633
  59.3 22.0 %collective-permute-start.4 = (bf16[256,768]{1,0:T(8,128)(2,1)S(1)}, bf16[256,768]{1,0:T(8,128)(2,1)S(1)}, u32[]{:S(2)}, u32[]{:S(2)}) collective-permute-start(bf16[256,768]{1,0:T(8,128)(2,1)S(1)} %bitcast.106), channel_id=1, source_target_pairs={{0,4},{1,5},{2,6},{3,7},{4,0},{5,1},{6,2},{7,3},{8,12},{9,13},{10,... | collective-permute-start | bytes 1179656 | tf_op jit(solution)/shard_map/ppermute | solution.py:627
  64.8 19.8 %collective-permute-start.5 = (bf16[256,768]{1,0:T(8,128)(2,1)S(1)}, bf16[256,768]{1,0:T(8,128)(2,1)S(1)}, u32[]{:S(2)}, u32[]{:S(2)}) collective-permute-start(bf16[256,768]{1,0:T(8,128)(2,1)S(1)} %bitcast.107), channel_id=1, source_target_pairs={{0,8},{1,9},{2,10},{3,11},{4,12},{5,13},{6,14},{7,15},{8,0},{9,1},... | collective-permute-start | bytes 1179656 | tf_op jit(solution)/shard_map/ppermute | solution.py:627
  72.7 43.4 %collective-permute-start.10 = (bf16[384,1024]{1,0:T(8,128)(2,1)}, bf16[384,1024]{1,0:T(8,128)(2,1)}, u32[]{:S(2)}, u32[]{:S(2)}) collective-permute-start(bf16[384,1024]{1,0:T(8,128)(2,1)} %get-tuple-element.75.refs_2_), channel_id=1, source_target_pairs={{0,3},{1,2},{2,1},{3,0},{4,7},{5,6},{6,5},{7,4},{8,11},{9,10},{10,... | collective-permute-start | bytes 2359304 | tf_op jit(solution)/shard_map/ppermute | solution.py:630
  75.3 40.8 %collective-permute-start.8 = (bf16[384,1024]{1,0:T(8,128)(2,1)}, bf16[384,1024]{1,0:T(8,128)(2,1)}, u32[]{:S(2)}, u32[]{:S(2)}) collective-permute-start(bf16[384,1024]{1,0:T(8,128)(2,1)} %get-tuple-element.75.refs_2_), channel_id=1, source_target_pairs={{0,1},{1,0},{2,3},{3,2},{4,5},{5,4},{6,7},{7,6},{8,9},{9,8},{10,11... | collective-permute-start | bytes 2359304 | tf_op jit(solution)/shard_map/ppermute | solution.py:630
  81.3 34.8 %collective-permute-start.9 = (bf16[384,1024]{1,0:T(8,128)(2,1)}, bf16[384,1024]{1,0:T(8,128)(2,1)}, u32[]{:S(2)}, u32[]{:S(2)}) collective-permute-start(bf16[384,1024]{1,0:T(8,128)(2,1)} %get-tuple-element.75.refs_2_), channel_id=1, source_target_pairs={{0,2},{1,3},{2,0},{3,1},{4,6},{5,7},{6,4},{7,5},{8,10},{9,11},{10,... | collective-permute-start | bytes 2359304 | tf_op jit(solution)/shard_map/ppermute | solution.py:630
  84.6 11.6 %collective-permute-start.6 = (bf16[256,768]{1,0:T(8,128)(2,1)S(1)}, bf16[256,768]{1,0:T(8,128)(2,1)S(1)}, u32[]{:S(2)}, u32[]{:S(2)}) collective-permute-start(bf16[256,768]{1,0:T(8,128)(2,1)S(1)} %bitcast.108), channel_id=1, source_target_pairs={{0,12},{1,13},{2,14},{3,15},{4,8},{5,9},{6,10},{7,11},{8,4},{9,5},... | collective-permute-start | bytes 1179656 | tf_op jit(solution)/shard_map/ppermute | solution.py:627
  116.1 3.1 %collective-permute-start.14 = (bf16[384,1536]{1,0:T(8,128)(2,1)}, bf16[384,1536]{1,0:T(8,128)(2,1)S(1)}, u32[]{:S(2)}, u32[]{:S(2)}) collective-permute-start(bf16[384,1536]{1,0:T(8,128)(2,1)} %get-tuple-element.87), channel_id=1, source_target_pairs={{0,16},{16,0},{1,17},{17,1},{2,18},{18,2},{3,19},{19,3},{4,20},{20... | collective-permute-start | bytes 3538952 | tf_op jit(solution)/shard_map/ppermute | solution.py:633
  121.8 34.7 %all-to-all-start.3 = ((bf16[4,96,1536]{2,1,0:T(8,128)(2,1)}), bf16[4,96,1536]{2,1,0:T(8,128)(2,1)S(1)}, u32[]{:S(2)}, u32[]{:S(2)}) async-start(bf16[4,96,1536]{2,1,0:T(8,128)(2,1)} %bitcast.35), calls=%async_computation.3 | async-start | bytes 2359296 | tf_op jit(solution)/shard_map/all_to_all | solution.py:639
  147.1 36.5 %collective-permute-start.11 = (bf16[256,768]{1,0:T(8,128)(2,1)}, bf16[256,768]{1,0:T(8,128)(2,1)S(1)}, u32[]{:S(2)}, u32[]{:S(2)}) collective-permute-start(bf16[256,768]{1,0:T(8,128)(2,1)} %get-tuple-element.80), channel_id=1, source_target_pairs={{0,4},{1,5},{2,6},{3,7},{4,0},{5,1},{6,2},{7,3},{8,12},{9,13},{10,... | collective-permute-start | bytes 1179656 | tf_op jit(solution)/shard_map/ppermute | solution.py:627
  154.0 30.1 %collective-permute-start.12 = (bf16[256,768]{1,0:T(8,128)(2,1)}, bf16[256,768]{1,0:T(8,128)(2,1)}, u32[]{:S(2)}, u32[]{:S(2)}) collective-permute-start(bf16[256,768]{1,0:T(8,128)(2,1)} %get-tuple-element.81), channel_id=1, source_target_pairs={{0,8},{1,9},{2,10},{3,11},{4,12},{5,13},{6,14},{7,15},{8,0},{9,1},... | collective-permute-start | bytes 1179656 | tf_op jit(solution)/shard_map/ppermute | solution.py:627
  154.2 29.9 %collective-permute-start.13 = (bf16[256,768]{1,0:T(8,128)(2,1)}, bf16[256,768]{1,0:T(8,128)(2,1)}, u32[]{:S(2)}, u32[]{:S(2)}) collective-permute-start(bf16[256,768]{1,0:T(8,128)(2,1)} %get-tuple-element.82), channel_id=1, source_target_pairs={{0,12},{1,13},{2,14},{3,15},{4,8},{5,9},{6,10},{7,11},{8,4},{9,5},... | collective-permute-start | bytes 1179656 | tf_op jit(solution)/shard_map/ppermute | solution.py:627
  156.5 27.6 %copy-start.7 = (f32[256,768]{1,0:T(8,128)S(1)}, f32[256,768]{1,0:T(8,128)}, u32[]{:S(2)}) copy-start(f32[256,768]{1,0:T(8,128)} %get-tuple-element.91) | copy-start | bytes 2359300
  186.3 21.5 %collective-permute-start.15 = (bf16[384,1024]{1,0:T(8,128)(2,1)}, bf16[384,1024]{1,0:T(8,128)(2,1)}, u32[]{:S(2)}, u32[]{:S(2)}) collective-permute-start(bf16[384,1024]{1,0:T(8,128)(2,1)} %get-tuple-element.106), channel_id=1, source_target_pairs={{0,1},{1,0},{2,3},{3,2},{4,5},{5,4},{6,7},{7,6},{8,9},{9,8},{10,11... | collective-permute-start | bytes 2359304 | tf_op jit(solution)/shard_map/ppermute | solution.py:630
  193.0 39.1 %collective-permute-start.16 = (bf16[384,1024]{1,0:T(8,128)(2,1)}, bf16[384,1024]{1,0:T(8,128)(2,1)}, u32[]{:S(2)}, u32[]{:S(2)}) collective-permute-start(bf16[384,1024]{1,0:T(8,128)(2,1)} %get-tuple-element.107), channel_id=1, source_target_pairs={{0,2},{1,3},{2,0},{3,1},{4,6},{5,7},{6,4},{7,5},{8,10},{9,11},{10,... | collective-permute-start | bytes 2359304 | tf_op jit(solution)/shard_map/ppermute | solution.py:630
  198.5 33.6 %collective-permute-start.17 = (bf16[384,1024]{1,0:T(8,128)(2,1)}, bf16[384,1024]{1,0:T(8,128)(2,1)}, u32[]{:S(2)}, u32[]{:S(2)}) collective-permute-start(bf16[384,1024]{1,0:T(8,128)(2,1)} %get-tuple-element.108), channel_id=1, source_target_pairs={{0,3},{1,2},{2,1},{3,0},{4,7},{5,6},{6,5},{7,4},{8,11},{9,10},{10,... | collective-permute-start | bytes 2359304 | tf_op jit(solution)/shard_map/ppermute | solution.py:630
  244.6 6.6 %collective-permute-start.18 = (bf16[384,1408]{1,0:T(8,128)(2,1)}, bf16[384,1408]{1,0:T(8,128)(2,1)}, u32[]{:S(2)}, u32[]{:S(2)}) collective-permute-start(bf16[384,1408]{1,0:T(8,128)(2,1)} %get-tuple-element.111), channel_id=1, source_target_pairs={{0,16},{16,0},{1,17},{17,1},{2,18},{18,2},{3,19},{19,3},{4,20},{20... | collective-permute-start | bytes 3244040 | tf_op jit(solution)/shard_map/ppermute | solution.py:633
  246.4 42.4 %all-to-all-start.4 = ((bf16[4,256,768]{2,1,0:T(8,128)(2,1)}), bf16[4,256,768]{2,1,0:T(8,128)(2,1)S(1)}, u32[]{:S(2)}, u32[]{:S(2)}) async-start(bf16[4,256,768]{2,1,0:T(8,128)(2,1)} %get-tuple-element.109), calls=%async_computation.4 | async-start | bytes 3145728 | tf_op jit(solution)/shard_map/all_to_all | solution.py:639
  254.9 9.6 %collective-permute-start.19 = (bf16[96,1408]{1,0:T(8,128)(2,1)}, bf16[96,1408]{1,0:T(8,128)(2,1)}, u32[]{:S(2)}, u32[]{:S(2)}) collective-permute-start(bf16[96,1408]{1,0:T(8,128)(2,1)} %get-tuple-element.121), channel_id=1, source_target_pairs={{0,1},{1,0},{2,3},{3,2},{4,5},{5,4},{6,7},{7,6},{8,9},{9,8},{10,11... | collective-permute-start | bytes 811016 | tf_op jit(solution)/shard_map/ppermute | solution.py:630
  256.4 12.6 %collective-permute-start.20 = (bf16[96,1408]{1,0:T(8,128)(2,1)}, bf16[96,1408]{1,0:T(8,128)(2,1)}, u32[]{:S(2)}, u32[]{:S(2)}) collective-permute-start(bf16[96,1408]{1,0:T(8,128)(2,1)} %get-tuple-element.123), channel_id=1, source_target_pairs={{0,2},{1,3},{2,0},{3,1},{4,6},{5,7},{6,4},{7,5},{8,10},{9,11},{10,... | collective-permute-start | bytes 811016 | tf_op jit(solution)/shard_map/ppermute | solution.py:630
  257.0 13.8 %collective-permute-start.21 = (bf16[96,1408]{1,0:T(8,128)(2,1)}, bf16[96,1408]{1,0:T(8,128)(2,1)}, u32[]{:S(2)}, u32[]{:S(2)}) collective-permute-start(bf16[96,1408]{1,0:T(8,128)(2,1)} %get-tuple-element.122), channel_id=1, source_target_pairs={{0,3},{1,2},{2,1},{3,0},{4,7},{5,6},{6,5},{7,4},{8,11},{9,10},{10,... | collective-permute-start | bytes 811016 | tf_op jit(solution)/shard_map/ppermute | solution.py:630
  288.9 8.4 %collective-permute-start.22 = (bf16[24,2176]{1,0:T(8,128)(2,1)S(1)}, bf16[24,2176]{1,0:T(8,128)(2,1)S(1)}, u32[]{:S(2)}, u32[]{:S(2)}) collective-permute-start(bf16[24,2176]{1,0:T(8,128)(2,1)S(1)} %get-tuple-element.126), channel_id=1, source_target_pairs={{0,4},{1,5},{2,6},{3,7},{4,0},{5,1},{6,2},{7,3},{8,12},{9,13},{10,... | collective-permute-start | bytes 313352 | tf_op jit(solution)/shard_map/ppermute | solution.py:627
  289.9 10.7 %collective-permute-start.23 = (bf16[24,2176]{1,0:T(8,128)(2,1)S(1)}, bf16[24,2176]{1,0:T(8,128)(2,1)S(1)}, u32[]{:S(2)}, u32[]{:S(2)}) collective-permute-start(bf16[24,2176]{1,0:T(8,128)(2,1)S(1)} %get-tuple-element.125), channel_id=1, source_target_pairs={{0,8},{1,9},{2,10},{3,11},{4,12},{5,13},{6,14},{7,15},{8,0},{9,1},... | collective-permute-start | bytes 313352 | tf_op jit(solution)/shard_map/ppermute | solution.py:627
  292.2 8.5 %collective-permute-start.24 = (bf16[24,2176]{1,0:T(8,128)(2,1)S(1)}, bf16[24,2176]{1,0:T(8,128)(2,1)S(1)}, u32[]{:S(2)}, u32[]{:S(2)}) collective-permute-start(bf16[24,2176]{1,0:T(8,128)(2,1)S(1)} %get-tuple-element.124), channel_id=1, source_target_pairs={{0,12},{1,13},{2,14},{3,15},{4,8},{5,9},{6,10},{7,11},{8,4},{9,5},... | collective-permute-start | bytes 313352 | tf_op jit(solution)/shard_map/ppermute | solution.py:627
  (28 other events, 210.4 us)
where the time goes:
time: 311 us; the launch traced here: 307 us
  waiting for transfers between devices  96.7 us (31%)
  Pallas kernels  91.6 us (29%)
  starting transfers between devices  70.8 us (23%)
  local copies, waits for them, and re-layouts  25.3 us (8%)
  other arithmetic  16.8 us (5%)
    pallas_call x2, Pallas kernels, attention_call(): pl.pallas_call(functools.partial(kernel, heads, groups, runs), out_shape=...  48.9 us
    all_to_all x5, waiting for transfers between devices, swapped(): lax.all_to_all(value, 'blk', 0, 0, axis_index_groups=lines, tiled=True)  41.4 us
    ppermute x9, waiting for transfers between devices, over_groups(): return lax.ppermute(value, 'blk', [(i, i ^ away) for i in range(members)])  37.9 us
    ppermute x12, starting transfers between devices, over_parts(): lax.ppermute(value, 'blk', [(i, i ^ away * groups) for i in range(members)])  26.2 us
    all_to_all x5, starting transfers between devices, swapped(): lax.all_to_all(value, 'blk', 0, 0, axis_index_groups=lines, tiled=True)  22.2 us
    ppermute x9, starting transfers between devices, over_groups(): return lax.ppermute(value, 'blk', [(i, i ^ away) for i in range(members)])  20.5 us
    pallas_call x1, Pallas kernels, feed(): pl.pallas_call(functools.partial(feed_kernel, heads), out_shape=(jax.Shap...  19.1 us
    ppermute x12, waiting for transfers between devices, over_parts(): lax.ppermute(value, 'blk', [(i, i ^ away * groups) for i in range(members)])  15.8 us
  transfers between devices with their start and end apart: 30, of which 14 were waited for; matrix products, arithmetic and copies ran while one was open for 9% of the time, Pallas kernels for 26%

commit v1 on v0

--- a/solution.py
+++ b/solution.py
@@ -128,6 +128,15 @@
         ref[...] = branch.astype(ref.dtype)
 
 
+def halves_of(groups, half):
+    steps = [2**k for k in range(groups.bit_length() - 1)]
+    steps = steps[::-1] if half else steps
+    kept = [0]
+    for away in steps[:-1]:
+        kept = kept + [source ^ away for source in kept]
+    return kept, [source ^ steps[-1] for source in kept], steps[::-1]
+
+
 def backward_kernel(
     heads,
     groups,
@@ -144,8 +153,8 @@
     q_grad_ref,
     *refs,
 ):
-    kv_grad_refs = refs[:groups]
-    total, first_w, second_w, q_total = refs[groups:]
+    kv_grad_refs = refs[:4]
+    total, first_w, second_w, q_total = refs[4:]
     pair = 2 * HD
     total[...] = jnp.zeros_like(total)
 
@@ -192,18 +201,22 @@
 
     lax.fori_loop(0, q_ref.shape[1] // TILE, tile_step, 0)
 
-    for source in range(groups):
-
-        def give(run, carry, source=source):
-            at = pl.multiple_of(k_runs_ref[source * runs + run] * RUN, RUN)
-            columns = pl.ds(pl.multiple_of(run * RUN, RUN), RUN)
-            rows = total[pl.ds(at, RUN), :].astype(low)
-            for head in range(heads):
-                part = slice(head * pair, (head + 1) * pair)
-                kv_grad_refs[source][part, columns] = rows[:, part].T
-            return carry
-
-        lax.fori_loop(0, runs, give, 0)
+    half_runs = runs // 2
+    for half in range(2):
+        kept, sent, _ = halves_of(groups, half)
+        for ref, sources in zip(kv_grad_refs[2 * half : 2 * half + 2], (kept, sent)):
+            for slot, source in enumerate(sources):
+
+                def give(run, carry, ref=ref, slot=slot, first=source * runs + half * half_runs):
+                    at = pl.multiple_of(k_runs_ref[first + run] * RUN, RUN)
+                    columns = pl.ds(pl.multiple_of(run * RUN, RUN), RUN)
+                    rows = total[pl.ds(at, RUN), :].astype(low)
+                    for head in range(heads):
+                        part = slice(head * pair, (head + 1) * pair)
+                        ref[slot, part, columns] = rows[:, part].T
+                    return carry
+
+                lax.fori_loop(0, half_runs, give, 0)
 
 
 def attention_call(kernel, name, tables, operands, out_shape, scratch, groups, work):
@@ -260,8 +273,8 @@
     keys = kv.shape[0]
     groups = keys // count
     out_shape = (jax.ShapeDtypeStruct((width, count), full),) + (
-        jax.ShapeDtypeStruct((2 * width, count), low),
-    ) * groups
+        jax.ShapeDtypeStruct((groups // 2, 2 * width, count // 2), low),
+    ) * 4
     scratch = [
         pltpu.VMEM((keys, 2 * width), full),
         pltpu.VMEM((width // HD, 2 * HD, 2 * TILE), low),
@@ -460,6 +473,7 @@
 ):
     x_refs, kv_refs, outs = refs[:TP], refs[TP:-5], refs[-5:]
     kept_ref, sent_ref, slope_ref, gradient, joined = outs
+    kv_pairs = (kv_refs[:2], kv_refs[2:])
     span = heads * HD
     block, width = x_refs[0].shape
     half_dims = ROT // 2
@@ -477,7 +491,9 @@
         key = slice(2 * head * HD, (2 * head + 1) * HD)
         value = slice((2 * head + 1) * HD, (2 * head + 2) * HD)
         key_grad, value_grad = (
-            functools.reduce(jnp.add, [ref[part, :].astype(full) for ref in kv_refs])
+            jnp.concatenate(
+                [kept[part, :] + sent[part, :].astype(full) for kept, sent in kv_pairs], axis=1
+            )
             for part in (key, value)
         )
         to_key = span + 2 * head * HD
@@ -858,7 +874,17 @@
     early = [nothing, nothing, feed_sums[0], feed_sums[1], jnp.sum(upstream, axis=0)]
     early = jnp.stack(early + [nothing] * 3)
     early = jnp.concatenate([early, expand_sum.T], axis=0)
-    kv_grads = [kv_totals[0]] + [over_groups(kv_totals[r], r) for r in range(1, groups)]
+    kv_grads = []
+    for half in range(2):
+        kept, sent = kv_totals[2 * half : 2 * half + 2]
+        kept = kept.astype(full)
+        for away in halves_of(groups, half)[2]:
+            sent = over_groups(sent, away)
+            if kept.shape[0] > 1:
+                kept = kept + sent.astype(full)
+                middle = kept.shape[0] // 2
+                kept, sent = kept[:middle], kept[middle:].astype(low)
+        kv_grads += [kept[0], sent[0]]
     final_kept, final_sent, slopes = finish(
         heads,
         my_part[None].astype(jnp.int32),

time: 311 us -> 307 us (0.987)
  waiting for transfers between devices: 96.7 us -> 89.5 us
  starting transfers between devices: 70.8 us -> 77 us
  Pallas kernels: 91.6 us -> 85.8 us
    ppermute x9 -> x10, waiting for transfers between devices: 37.9 us -> 25.1 us  [over_groups(): return lax.ppermute(value, 'blk', [(i, i ^ away) for i in range(members)])]
    ppermute x9 -> x10, starting transfers between devices: 20.5 us -> 29.7 us  [over_groups(): return lax.ppermute(value, 'blk', [(i, i ^ away) for i in range(members)])]
    pallas_call x2, Pallas kernels: 48.9 us -> 43.9 us  [attention_call(): pl.pallas_call(functools.partial(kernel, heads, groups, runs), out_shape=...]
    ppermute x12, waiting for transfers between devices: 15.8 us -> 20.2 us  [over_parts(): lax.ppermute(value, 'blk', [(i, i ^ away * groups) for i in range(members)])]
  transfers between devices with their start and end apart: 30 -> 31, of which waited for: 14 -> 15; matrix products, arithmetic and copies ran while one was open for 9% -> 10% of each run, Pallas kernels for 26% -> 24%
where the time goes in v1:
time: 307 us; the launch traced here: 305 us
  waiting for transfers between devices  89.5 us (29%)
  Pallas kernels  85.8 us (28%)
  starting transfers between devices  77 us (25%)
  local copies, waits for them, and re-layouts  28.1 us (9%)
  other arithmetic  18.3 us (6%)
  matrix products  3.31 us (1%)
    pallas_call x2, Pallas kernels, attention_call(): pl.pallas_call(functools.partial(kernel, heads, groups, runs), out_shape=...  43.9 us
    all_to_all x5, waiting for transfers between devices, swapped(): lax.all_to_all(value, 'blk', 0, 0, axis_index_groups=lines, tiled=True)  42.5 us
    ppermute x10, starting transfers between devices, over_groups(): return lax.ppermute(value, 'blk', [(i, i ^ away) for i in range(members)])  29.7 us
    ppermute x12, starting transfers between devices, over_parts(): lax.ppermute(value, 'blk', [(i, i ^ away * groups) for i in range(members)])  26.2 us
    ppermute x10, waiting for transfers between devices, over_groups(): return lax.ppermute(value, 'blk', [(i, i ^ away) for i in range(members)])  25.1 us
    all_to_all x5, starting transfers between devices, swapped(): lax.all_to_all(value, 'blk', 0, 0, axis_index_groups=lines, tiled=True)  21 us
    ppermute x12, waiting for transfers between devices, over_parts(): lax.ppermute(value, 'blk', [(i, i ^ away * groups) for i in range(members)])  20.2 us
    pallas_call x1, Pallas kernels, feed(): pl.pallas_call(functools.partial(feed_kernel, heads), out_shape=(jax.Shap...  19 us
  transfers between devices with their start and end apart: 31, of which 15 were waited for; matrix products, arithmetic and copies ran while one was open for 10% of the time, Pallas kernels for 24%

profile of v1, /device:TPU:0, one launch (start us, length us, event | category | flops | bytes accessed | tf_op | source)
XLA Modules:
  0.0 305.0 jit_solution(18254575493465003506)
XLA Ops:
  5.3 6.3 %all-to-all-start = ((bf16[4,24,2176]{2,1,0:T(8,128)(2,1)}), bf16[4,24,2176]{2,1,0:T(8,128)(2,1)S(1)}, u32[]{:S(2)}, u32[]{:S(2)}) async-start(bf16[4,24,2176]{2,1,0:T(8,128)(2,1)} %concatenate.29), calls=%async_computation | async-start | bytes 835584 | tf_op jit(solution)/shard_map/all_to_all | solution.py:655
  18.3 5.4 %all-to-all-done = bf16[4,24,2176]{2,1,0:T(8,128)(2,1)S(1)} async-done(((bf16[4,24,2176]{2,1,0:T(8,128)(2,1)}), bf16[4,24,2176]{2,1,0:T(8,128)(2,1)S(1)}, u32[]{:S(2)}, u32[]{:S(2)}) %all-to-all-start) | async-done | bytes 417824 | tf_op jit(solution)/shard_map/all_to_all | solution.py:655
  24.5 3.7 %all-to-all-start.1 = ((bf16[4,96,640]{2,1,0:T(8,128)(2,1)}), bf16[4,96,640]{2,1,0:T(8,128)(2,1)S(1)}, u32[]{:S(2)}, u32[]{:S(2)}) async-start(bf16[4,96,640]{2,1,0:T(8,128)(2,1)} %broadcast_in_dim.73), calls=%async_computation.1 | async-start | bytes 983040 | tf_op jit(solution)/shard_map/all_to_all | solution.py:655
  29.3 3.2 %collective-permute-start.2 = (bf16[256,768]{1,0:T(8,128)(2,1)S(1)}, bf16[256,768]{1,0:T(8,128)(2,1)}, u32[]{:S(2)}, u32[]{:S(2)}) collective-permute-start(bf16[256,768]{1,0:T(8,128)(2,1)S(1)} %select_bitcast_fusion.refs_0_.x_ref), channel_id=1, source_target_pairs={{0,12},{1,13},{2,14},{3,15},{4,8},{5,9},{6,10},{7,11},{8,4},{9,5},... | collective-permute-start | bytes 1179656 | tf_op jit(solution)/shard_map/ppermute | solution.py:643
  36.1 3.9 %all-to-all-start.2 = ((bf16[4,96,2304]{2,1,0:T(8,128)(2,1)}), bf16[4,96,2304]{2,1,0:T(8,128)(2,1)S(1)}, u32[]{:S(2)}, u32[]{:S(2)}) async-start(bf16[4,96,2304]{2,1,0:T(8,128)(2,1)} %broadcast_in_dim.78), calls=%async_computation.2 | async-start | bytes 3538944 | tf_op jit(solution)/shard_map/all_to_all | solution.py:655
  41.1 17.2 %all-to-all-done.2 = bf16[4,96,2304]{2,1,0:T(8,128)(2,1)S(1)} async-done(((bf16[4,96,2304]{2,1,0:T(8,128)(2,1)}), bf16[4,96,2304]{2,1,0:T(8,128)(2,1)S(1)}, u32[]{:S(2)}, u32[]{:S(2)}) %all-to-all-start.2) | async-done | bytes 1769504 | tf_op jit(solution)/shard_map/all_to_all | solution.py:655
  59.3 5.5 %collective-permute-start.4 = (bf16[256,768]{1,0:T(8,128)(2,1)S(1)}, bf16[256,768]{1,0:T(8,128)(2,1)S(1)}, u32[]{:S(2)}, u32[]{:S(2)}) collective-permute-start(bf16[256,768]{1,0:T(8,128)(2,1)S(1)} %bitcast.112), channel_id=1, source_target_pairs={{0,4},{1,5},{2,6},{3,7},{4,0},{5,1},{6,2},{7,3},{8,12},{9,13},{10,... | collective-permute-start | bytes 1179656 | tf_op jit(solution)/shard_map/ppermute | solution.py:643
  64.8 7.9 %prepare.1 = (bf16[192,1024]{1,0:T(8,128)(2,1)}, bf16[384,1024]{1,0:T(8,128)(2,1)}, bf16[1024,768]{1,0:T(8,128)(2,1)}, bf16[1024,768]{1,0:T(8,128)(2,1)}, bf16[576,768]{1,0:T(8,128)(2,1)}, /*index=5*/f32[64,768]{1,0:T(8,128)}) custom-call(bf16[768,768]{1,0:T(8,128)(2,1)} %get-tuple-element.139.order_ref, s32[576,1]{1,0:T(8,128)} %copy.86.source_ref, ...), custom_call_target="tpu_custom_call" | custom-call | flops 7549747200 | bytes 12582912 | tf_op jit(solution)/shard_map/prepare/pallas_call | solution.py:350
  72.7 2.6 collective-permute-start.10
  75.8 5.5 %collective-permute-done.4.refs_5_ = bf16[256,768]{1,0:T(8,128)(2,1)S(1)} collective-permute-done((bf16[256,768]{1,0:T(8,128)(2,1)S(1)}, bf16[256,768]{1,0:T(8,128)(2,1)S(1)}, u32[]{:S(2)}, u32[]{:S(2)}) %collective-permute-start.4) | collective-permute-done | bytes 393248 | tf_op jit(solution)/shard_map/ppermute | solution.py:643
  89.7 6.4 %collective-permute-done.6.refs_7_ = bf16[256,768]{1,0:T(8,128)(2,1)S(1)} collective-permute-done((bf16[256,768]{1,0:T(8,128)(2,1)S(1)}, bf16[256,768]{1,0:T(8,128)(2,1)S(1)}, u32[]{:S(2)}, u32[]{:S(2)}) %collective-permute-start.6) | collective-permute-done | bytes 393248 | tf_op jit(solution)/shard_map/ppermute | solution.py:643
  96.9 19.0 %feed.1 = (bf16[192,1024]{1,0:T(8,128)(2,1)}, bf16[192,768]{1,0:T(8,128)(2,1)}, f32[1024,768]{1,0:T(8,128)}, f32[1024,768]{1,0:T(8,128)}, f32[8,768]{1,0:T(8,128...) custom-call(s32[1]{0:T(128)} %bitcast.30.part_ref, bf16[768,768]{1,0:T(8,128)(2,1)} %get-tuple-element.139.order_ref, ...), custom_call_target="tpu_custom_call" | custom-call | tf_op jit(solution)/shard_map/feed/pallas_call | solution.py:432
  119.1 2.6 add_convert_fusion
  121.7 3.5 %all-to-all-start.3 = ((bf16[4,96,1536]{2,1,0:T(8,128)(2,1)}), bf16[4,96,1536]{2,1,0:T(8,128)(2,1)S(1)}, u32[]{:S(2)}, u32[]{:S(2)}) async-start(bf16[4,96,1536]{2,1,0:T(8,128)(2,1)} %bitcast.35), calls=%async_computation.3 | async-start | bytes 2359296 | tf_op jit(solution)/shard_map/all_to_all | solution.py:655
  125.2 20.9 %attend.1 = (bf16[192,1024]{1,0:T(8,128)(2,1)}, bf16[4096,384]{1,0:T(8,128)(2,1)}, bf16[384,4096]{1,0:T(8,128)(2,1)}, f32[8,1024]{1,0:T(8,128)}, f32[8,1024]{1,0...) custom-call(s32[8]{0:T(128)} %copy-done.19, ...), custom_call_target="tpu_custom_call" | custom-call | flops 37748736000 | bytes 6291456 | tf_op jit(solution)/shard_map/attend/pallas_call | solution.py:228
  146.1 6.9 %collective-permute-start.11 = (bf16[256,768]{1,0:T(8,128)(2,1)}, bf16[256,768]{1,0:T(8,128)(2,1)S(1)}, u32[]{:S(2)}, u32[]{:S(2)}) collective-permute-start(bf16[256,768]{1,0:T(8,128)(2,1)} %get-tuple-element.80), channel_id=1, source_target_pairs={{0,4},{1,5},{2,6},{3,7},{4,0},{5,1},{6,2},{7,3},{8,12},{9,13},{10,... | collective-permute-start | bytes 1179656 | tf_op jit(solution)/shard_map/ppermute | solution.py:643
  155.4 23.1 %attend_back.1 = (f32[192,1024]{1,0:T(8,128)}, bf16[2,384,512]{2,1,0:T(8,128)(2,1)}, bf16[2,384,512]{2,1,0:T(8,128)(2,1)}, bf16[2,384,512]{2,1,0:T(8,128)(2,1)}, bf16[2,384,512]{2,1,0:T(8,128)(2,1)}) custom-call(s32[8]{0:T(128)} %copy-done.19, s32[8]{0:T(128)} %select_reduce_fusion.q_order_ref, s32[32]{0:T(128)} %reshape_reshape.3.k_runs_ref, ...), custom_call_target="tpu_custom_call" | custom-call | flops 37748736000 | bytes 6291456 | tf_op jit(solution)/shard_map/attend_back/pallas_call | solution.py:228
  178.4 4.6 %collective-permute-done.12 = bf16[256,768]{1,0:T(8,128)(2,1)} collective-permute-done((bf16[256,768]{1,0:T(8,128)(2,1)}, bf16[256,768]{1,0:T(8,128)(2,1)}, u32[]{:S(2)}, u32[]{:S(2)}) %collective-permute-start.12) | collective-permute-done | bytes 393248 | tf_op jit(solution)/shard_map/ppermute | solution.py:643
  185.2 21.2 %collective-permute-start.17 = (bf16[2,384,512]{2,1,0:T(8,128)(2,1)}, bf16[2,384,512]{2,1,0:T(8,128)(2,1)S(1)}, u32[]{:S(2)}, u32[]{:S(2)}) collective-permute-start(bf16[2,384,512]{2,1,0:T(8,128)(2,1)} %get-tuple-element.108), channel_id=1, source_target_pairs={{0,1},{1,0},{2,3},{3,2},{4,5},{5,4},{6,7},{7,6},{8,9},{9,8},{10,11... | collective-permute-start | bytes 2359304 | tf_op jit(solution)/shard_map/ppermute | solution.py:646
  211.5 3.3 %convolution_convert_fusion.merge_ref = bf16[768,768]{1,0:T(8,128)(2,1)} fusion(bf16[192,1024]{1,0:T(8,128)(2,1)} %get-tuple-element.104, bf16[256,768]{1,0:T(8,128)(2,1)} %copy-done.13, bf16[256,768]{1,0:T(8,128)(2,1)} %collective-permute-done.5.refs_6_, bf16[256,768]{1,0:T(8,128)(2,1)S(1)} %copy-done.12, bf16[256,768]{1,0:T(8,128)(2,1)S(1)} %bitcast.115, ...), kind=kOutput, calls=%fused_computation.20 | convolution fusion | flops 535511040 | bytes 3293188 | tf_op jit(solution)/shard_map/dot_general | solution.py:27
  214.8 2.9 collective-permute-done.17
  218.0 5.1 %collective-permute-done.15 = bf16[2,384,512]{2,1,0:T(8,128)(2,1)} collective-permute-done((bf16[2,384,512]{2,1,0:T(8,128)(2,1)}, bf16[2,384,512]{2,1,0:T(8,128)(2,1)}, u32[]{:S(2)}, u32[]{:S(2)}) %collective-permute-start.15) | collective-permute-done | bytes 786464 | tf_op jit(solution)/shard_map/ppermute | solution.py:646
  227.3 5.1 %collective-permute-done.16 = bf16[1,384,512]{2,1,0:T(8,128)(2,1)S(1)} collective-permute-done((bf16[1,384,512]{2,1,0:T(8,128)(2,1)S(1)}, bf16[1,384,512]{2,1,0:T(8,128)(2,1)S(1)}, u32[]{:S(2)}, u32[]{:S(2)}) %collective-permute-start.16) | collective-permute-done | bytes 393248 | tf_op jit(solution)/shard_map/ppermute | solution.py:646
  233.2 11.8 %finish.1 = (bf16[384,1408]{1,0:T(8,128)(2,1)}, bf16[384,1408]{1,0:T(8,128)(2,1)}, bf16[4,256,768]{2,1,0:T(8,128)(2,1)}) custom-call(s32[1]{0:T(128)} %bitcast.30.part_ref, bf16[768,768]{1,0:T(8,128)(2,1)} %get-tuple-element.140.back_order_ref.order_ref, s32[768,1]{1,0:T(8,128)} %fusion.32.place_ref, s32[1,576]{1,0:T(1,128)} %copy-done.17, ...), custom_call_target="tpu_custom_call" | custom-call | flops 7549747200 | bytes 12582912 | tf_op jit(solution)/shard_map/finish/pallas_call | solution.py:558
  245.0 3.6 %all-to-all-start.4 = ((bf16[4,256,768]{2,1,0:T(8,128)(2,1)}), bf16[4,256,768]{2,1,0:T(8,128)(2,1)S(1)}, u32[]{:S(2)}, u32[]{:S(2)}) async-start(bf16[4,256,768]{2,1,0:T(8,128)(2,1)} %get-tuple-element.109), calls=%async_computation.4 | async-start | bytes 3145728 | tf_op jit(solution)/shard_map/all_to_all | solution.py:655
  252.3 3.5 %collective-permute-start.22 = (bf16[96,1408]{1,0:T(8,128)(2,1)}, bf16[96,1408]{1,0:T(8,128)(2,1)}, u32[]{:S(2)}, u32[]{:S(2)}) collective-permute-start(bf16[96,1408]{1,0:T(8,128)(2,1)} %get-tuple-element.122), channel_id=1, source_target_pairs={{0,3},{1,2},{2,1},{3,0},{4,7},{5,6},{6,5},{7,4},{8,11},{9,10},{10,... | collective-permute-start | bytes 811016 | tf_op jit(solution)/shard_map/ppermute | solution.py:646
  256.0 5.9 %collective-permute-done.20 = bf16[96,1408]{1,0:T(8,128)(2,1)} collective-permute-done((bf16[96,1408]{1,0:T(8,128)(2,1)}, bf16[96,1408]{1,0:T(8,128)(2,1)}, u32[]{:S(2)}, u32[]{:S(2)}) %collective-permute-start.20) | collective-permute-done | bytes 270368 | tf_op jit(solution)/shard_map/ppermute | solution.py:646
  261.9 5.4 %collective-permute-done.21 = bf16[96,1408]{1,0:T(8,128)(2,1)} collective-permute-done((bf16[96,1408]{1,0:T(8,128)(2,1)}, bf16[96,1408]{1,0:T(8,128)(2,1)}, u32[]{:S(2)}, u32[]{:S(2)}) %collective-permute-start.21) | collective-permute-done | bytes 270368 | tf_op jit(solution)/shard_map/ppermute | solution.py:646
  268.6 17.8 %all-to-all-done.4.slopes_ref = bf16[4,256,768]{2,1,0:T(8,128)(2,1)S(1)} async-done(((bf16[4,256,768]{2,1,0:T(8,128)(2,1)}), bf16[4,256,768]{2,1,0:T(8,128)(2,1)S(1)}, u32[]{:S(2)}, u32[]{:S(2)}) %all-to-all-start.4) | async-done | bytes 1572896 | tf_op jit(solution)/shard_map/all_to_all | solution.py:655
  289.3 2.4 collective-permute-start.25
  291.7 3.2 %tokens_gradient.1 = f32[256,768]{1,0:T(8,128)} custom-call(bf16[256,768]{1,0:T(8,128)(2,1)} %copy-done.5, bf16[256,768]{1,0:T(8,128)(2,1)} %bitcast.111, bf16[4,256,768]{2,1,0:T(8,128)(2,1)} %copy-done.1), custom_call_target="tpu_custom_call" | custom-call | tf_op jit(solution)/shard_map/tokens_gradient/pallas_call | solution.py:604
  294.9 3.6 %collective-permute-done.24 = bf16[24,2176]{1,0:T(8,128)(2,1)S(1)} collective-permute-done((bf16[24,2176]{1,0:T(8,128)(2,1)S(1)}, bf16[24,2176]{1,0:T(8,128)(2,1)S(1)}, u32[]{:S(2)}, u32[]{:S(2)}) %collective-permute-start.24) | collective-permute-done | bytes 104480 | tf_op jit(solution)/shard_map/ppermute | solution.py:643
  (227 shorter events, 59.1 us)
Async XLA Ops:
  5.3 18.4 %all-to-all-start = ((bf16[4,24,2176]{2,1,0:T(8,128)(2,1)}), bf16[4,24,2176]{2,1,0:T(8,128)(2,1)S(1)}, u32[]{:S(2)}, u32[]{:S(2)}) async-start(bf16[4,24,2176]{2,1,0:T(8,128)(2,1)} %concatenate.29), calls=%async_computation | async-start | bytes 835584 | tf_op jit(solution)/shard_map/all_to_all | solution.py:655
  13.5 45.8 %collective-permute-start = (bf16[256,768]{1,0:T(8,128)(2,1)S(1)}, bf16[256,768]{1,0:T(8,128)(2,1)}, u32[]{:S(2)}, u32[]{:S(2)}) collective-permute-start(bf16[256,768]{1,0:T(8,128)(2,1)S(1)} %select_bitcast_fusion.refs_0_.x_ref), channel_id=1, source_target_pairs={{0,4},{1,5},{2,6},{3,7},{4,0},{5,1},{6,2},{7,3},{8,12},{9,13},{10,... | collective-permute-start | bytes 1179656 | tf_op jit(solution)/shard_map/ppermute | solution.py:643
  24.5 10.1 %all-to-all-start.1 = ((bf16[4,96,640]{2,1,0:T(8,128)(2,1)}), bf16[4,96,640]{2,1,0:T(8,128)(2,1)S(1)}, u32[]{:S(2)}, u32[]{:S(2)}) async-start(bf16[4,96,640]{2,1,0:T(8,128)(2,1)} %broadcast_in_dim.73), calls=%async_computation.1 | async-start | bytes 983040 | tf_op jit(solution)/shard_map/all_to_all | solution.py:655
  29.3 30.0 %collective-permute-start.1 = (bf16[256,768]{1,0:T(8,128)(2,1)S(1)}, bf16[256,768]{1,0:T(8,128)(2,1)}, u32[]{:S(2)}, u32[]{:S(2)}) collective-permute-start(bf16[256,768]{1,0:T(8,128)(2,1)S(1)} %select_bitcast_fusion.refs_0_.x_ref), channel_id=1, source_target_pairs={{0,8},{1,9},{2,10},{3,11},{4,12},{5,13},{6,14},{7,15},{8,0},{9,1},... | collective-permute-start | bytes 1179656 | tf_op jit(solution)/shard_map/ppermute | solution.py:643
  29.3 30.0 %collective-permute-start.2 = (bf16[256,768]{1,0:T(8,128)(2,1)S(1)}, bf16[256,768]{1,0:T(8,128)(2,1)}, u32[]{:S(2)}, u32[]{:S(2)}) collective-permute-start(bf16[256,768]{1,0:T(8,128)(2,1)S(1)} %select_bitcast_fusion.refs_0_.x_ref), channel_id=1, source_target_pairs={{0,12},{1,13},{2,14},{3,15},{4,8},{5,9},{6,10},{7,11},{8,4},{9,5},... | collective-permute-start | bytes 1179656 | tf_op jit(solution)/shard_map/ppermute | solution.py:643
  36.1 22.2 %all-to-all-start.2 = ((bf16[4,96,2304]{2,1,0:T(8,128)(2,1)}), bf16[4,96,2304]{2,1,0:T(8,128)(2,1)S(1)}, u32[]{:S(2)}, u32[]{:S(2)}) async-start(bf16[4,96,2304]{2,1,0:T(8,128)(2,1)} %broadcast_in_dim.78), calls=%async_computation.2 | async-start | bytes 3538944 | tf_op jit(solution)/shard_map/all_to_all | solution.py:655
  40.7 24.1 %collective-permute-start.3 = (bf16[384,640]{1,0:T(8,128)(2,1)S(1)}, bf16[384,640]{1,0:T(8,128)(2,1)}, u32[]{:S(2)}, u32[]{:S(2)}) collective-permute-start(bf16[384,640]{1,0:T(8,128)(2,1)S(1)} %bitcast.122), channel_id=1, source_target_pairs={{0,16},{16,0},{1,17},{17,1},{2,18},{18,2},{3,19},{19,3},{4,20},{20... | collective-permute-start | bytes 1474568 | tf_op jit(solution)/shard_map/ppermute | solution.py:649
  41.0 75.7 %copy-start.19 = (s32[8]{0:T(128)}, s32[8]{0:T(128)S(1)}, u32[]{:S(2)}) copy-start(s32[8]{0:T(128)S(1)} %squeeze.58.q_runs_ref) | copy-start | bytes 100
  58.2 37.9 %collective-permute-start.7 = (bf16[384,2304]{1,0:T(8,128)(2,1)S(1)}, bf16[384,2304]{1,0:T(8,128)(2,1)}, u32[]{:S(2)}, u32[]{:S(2)}) collective-permute-start(bf16[384,2304]{1,0:T(8,128)(2,1)S(1)} %bitcast.106), channel_id=1, source_target_pairs={{0,16},{16,0},{1,17},{17,1},{2,18},{18,2},{3,19},{19,3},{4,20},{20... | collective-permute-start | bytes 5308424 | tf_op jit(solution)/shard_map/ppermute | solution.py:649
  59.3 22.0 %collective-permute-start.4 = (bf16[256,768]{1,0:T(8,128)(2,1)S(1)}, bf16[256,768]{1,0:T(8,128)(2,1)S(1)}, u32[]{:S(2)}, u32[]{:S(2)}) collective-permute-start(bf16[256,768]{1,0:T(8,128)(2,1)S(1)} %bitcast.112), channel_id=1, source_target_pairs={{0,4},{1,5},{2,6},{3,7},{4,0},{5,1},{6,2},{7,3},{8,12},{9,13},{10,... | collective-permute-start | bytes 1179656 | tf_op jit(solution)/shard_map/ppermute | solution.py:643
  64.8 19.8 %collective-permute-start.5 = (bf16[256,768]{1,0:T(8,128)(2,1)S(1)}, bf16[256,768]{1,0:T(8,128)(2,1)}, u32[]{:S(2)}, u32[]{:S(2)}) collective-permute-start(bf16[256,768]{1,0:T(8,128)(2,1)S(1)} %bitcast.113), channel_id=1, source_target_pairs={{0,8},{1,9},{2,10},{3,11},{4,12},{5,13},{6,14},{7,15},{8,0},{9,1},... | collective-permute-start | bytes 1179656 | tf_op jit(solution)/shard_map/ppermute | solution.py:643
  72.7 43.3 %collective-permute-start.10 = (bf16[384,1024]{1,0:T(8,128)(2,1)}, bf16[384,1024]{1,0:T(8,128)(2,1)}, u32[]{:S(2)}, u32[]{:S(2)}) collective-permute-start(bf16[384,1024]{1,0:T(8,128)(2,1)} %get-tuple-element.75.refs_2_), channel_id=1, source_target_pairs={{0,3},{1,2},{2,1},{3,0},{4,7},{5,6},{6,5},{7,4},{8,11},{9,10},{10,... | collective-permute-start | bytes 2359304 | tf_op jit(solution)/shard_map/ppermute | solution.py:646
  75.2 40.7 %collective-permute-start.8 = (bf16[384,1024]{1,0:T(8,128)(2,1)}, bf16[384,1024]{1,0:T(8,128)(2,1)}, u32[]{:S(2)}, u32[]{:S(2)}) collective-permute-start(bf16[384,1024]{1,0:T(8,128)(2,1)} %get-tuple-element.75.refs_2_), channel_id=1, source_target_pairs={{0,1},{1,0},{2,3},{3,2},{4,5},{5,4},{6,7},{7,6},{8,9},{9,8},{10,11... | collective-permute-start | bytes 2359304 | tf_op jit(solution)/shard_map/ppermute | solution.py:646
  81.3 34.7 %collective-permute-start.9 = (bf16[384,1024]{1,0:T(8,128)(2,1)}, bf16[384,1024]{1,0:T(8,128)(2,1)}, u32[]{:S(2)}, u32[]{:S(2)}) collective-permute-start(bf16[384,1024]{1,0:T(8,128)(2,1)} %get-tuple-element.75.refs_2_), channel_id=1, source_target_pairs={{0,2},{1,3},{2,0},{3,1},{4,6},{5,7},{6,4},{7,5},{8,10},{9,11},{10,... | collective-permute-start | bytes 2359304 | tf_op jit(solution)/shard_map/ppermute | solution.py:646
  84.6 11.6 %collective-permute-start.6 = (bf16[256,768]{1,0:T(8,128)(2,1)S(1)}, bf16[256,768]{1,0:T(8,128)(2,1)S(1)}, u32[]{:S(2)}, u32[]{:S(2)}) collective-permute-start(bf16[256,768]{1,0:T(8,128)(2,1)S(1)} %bitcast.114), channel_id=1, source_target_pairs={{0,12},{1,13},{2,14},{3,15},{4,8},{5,9},{6,10},{7,11},{8,4},{9,5},... | collective-permute-start | bytes 1179656 | tf_op jit(solution)/shard_map/ppermute | solution.py:643
  116.0 3.1 %collective-permute-start.14 = (bf16[384,1536]{1,0:T(8,128)(2,1)}, bf16[384,1536]{1,0:T(8,128)(2,1)S(1)}, u32[]{:S(2)}, u32[]{:S(2)}) collective-permute-start(bf16[384,1536]{1,0:T(8,128)(2,1)} %get-tuple-element.87), channel_id=1, source_target_pairs={{0,16},{16,0},{1,17},{17,1},{2,18},{18,2},{3,19},{19,3},{4,20},{20... | collective-permute-start | bytes 3538952 | tf_op jit(solution)/shard_map/ppermute | solution.py:649
  121.7 33.7 %all-to-all-start.3 = ((bf16[4,96,1536]{2,1,0:T(8,128)(2,1)}), bf16[4,96,1536]{2,1,0:T(8,128)(2,1)S(1)}, u32[]{:S(2)}, u32[]{:S(2)}) async-start(bf16[4,96,1536]{2,1,0:T(8,128)(2,1)} %bitcast.35), calls=%async_computation.3 | async-start | bytes 2359296 | tf_op jit(solution)/shard_map/all_to_all | solution.py:655
  146.1 32.4 %collective-permute-start.11 = (bf16[256,768]{1,0:T(8,128)(2,1)}, bf16[256,768]{1,0:T(8,128)(2,1)S(1)}, u32[]{:S(2)}, u32[]{:S(2)}) collective-permute-start(bf16[256,768]{1,0:T(8,128)(2,1)} %get-tuple-element.80), channel_id=1, source_target_pairs={{0,4},{1,5},{2,6},{3,7},{4,0},{5,1},{6,2},{7,3},{8,12},{9,13},{10,... | collective-permute-start | bytes 1179656 | tf_op jit(solution)/shard_map/ppermute | solution.py:643
  153.0 30.1 %collective-permute-start.12 = (bf16[256,768]{1,0:T(8,128)(2,1)}, bf16[256,768]{1,0:T(8,128)(2,1)}, u32[]{:S(2)}, u32[]{:S(2)}) collective-permute-start(bf16[256,768]{1,0:T(8,128)(2,1)} %get-tuple-element.81), channel_id=1, source_target_pairs={{0,8},{1,9},{2,10},{3,11},{4,12},{5,13},{6,14},{7,15},{8,0},{9,1},... | collective-permute-start | bytes 1179656 | tf_op jit(solution)/shard_map/ppermute | solution.py:643
  153.1 30.0 %collective-permute-start.13 = (bf16[256,768]{1,0:T(8,128)(2,1)}, bf16[256,768]{1,0:T(8,128)(2,1)}, u32[]{:S(2)}, u32[]{:S(2)}) collective-permute-start(bf16[256,768]{1,0:T(8,128)(2,1)} %get-tuple-element.82), channel_id=1, source_target_pairs={{0,12},{1,13},{2,14},{3,15},{4,8},{5,9},{6,10},{7,11},{8,4},{9,5},... | collective-permute-start | bytes 1179656 | tf_op jit(solution)/shard_map/ppermute | solution.py:643
  185.2 32.4 %collective-permute-start.17 = (bf16[2,384,512]{2,1,0:T(8,128)(2,1)}, bf16[2,384,512]{2,1,0:T(8,128)(2,1)S(1)}, u32[]{:S(2)}, u32[]{:S(2)}) collective-permute-start(bf16[2,384,512]{2,1,0:T(8,128)(2,1)} %get-tuple-element.108), channel_id=1, source_target_pairs={{0,1},{1,0},{2,3},{3,2},{4,5},{5,4},{6,7},{7,6},{8,9},{9,8},{10,11... | collective-permute-start | bytes 2359304 | tf_op jit(solution)/shard_map/ppermute | solution.py:646
  206.6 16.6 %collective-permute-start.15 = (bf16[2,384,512]{2,1,0:T(8,128)(2,1)}, bf16[2,384,512]{2,1,0:T(8,128)(2,1)}, u32[]{:S(2)}, u32[]{:S(2)}) collective-permute-start(bf16[2,384,512]{2,1,0:T(8,128)(2,1)} %get-tuple-element.106), channel_id=1, source_target_pairs={{0,2},{1,3},{2,0},{3,1},{4,6},{5,7},{6,4},{7,5},{8,10},{9,11},{10,... | collective-permute-start | bytes 2359304 | tf_op jit(solution)/shard_map/ppermute | solution.py:646
  218.0 9.3 %collective-permute-start.18 = (bf16[1,384,512]{2,1,0:T(8,128)(2,1)S(1)}, bf16[1,384,512]{2,1,0:T(8,128)(2,1)S(1)}, u32[]{:S(2)}, u32[]{:S(2)}) collective-permute-start(bf16[1,384,512]{2,1,0:T(8,128)(2,1)S(1)} %slice.227), channel_id=1, source_target_pairs={{0,2},{1,3},{2,0},{3,1},{4,6},{5,7},{6,4},{7,5},{8,10},{9,11},{10,... | collective-permute-start | bytes 1179656 | tf_op jit(solution)/shard_map/ppermute | solution.py:646
  224.6 7.8 %collective-permute-start.16 = (bf16[1,384,512]{2,1,0:T(8,128)(2,1)S(1)}, bf16[1,384,512]{2,1,0:T(8,128)(2,1)S(1)}, u32[]{:S(2)}, u32[]{:S(2)}) collective-permute-start(bf16[1,384,512]{2,1,0:T(8,128)(2,1)S(1)} %slice.228), channel_id=1, source_target_pairs={{0,1},{1,0},{2,3},{3,2},{4,5},{5,4},{6,7},{7,6},{8,9},{9,8},{10,11... | collective-permute-start | bytes 1179656 | tf_op jit(solution)/shard_map/ppermute | solution.py:646
  244.9 3.6 %collective-permute-start.19 = (bf16[384,1408]{1,0:T(8,128)(2,1)}, bf16[384,1408]{1,0:T(8,128)(2,1)}, u32[]{:S(2)}, u32[]{:S(2)}) collective-permute-start(bf16[384,1408]{1,0:T(8,128)(2,1)} %get-tuple-element.111), channel_id=1, source_target_pairs={{0,16},{16,0},{1,17},{17,1},{2,18},{18,2},{3,19},{19,3},{4,20},{20... | collective-permute-start | bytes 3244040 | tf_op jit(solution)/shard_map/ppermute | solution.py:649
  245.0 41.4 %all-to-all-start.4 = ((bf16[4,256,768]{2,1,0:T(8,128)(2,1)}), bf16[4,256,768]{2,1,0:T(8,128)(2,1)S(1)}, u32[]{:S(2)}, u32[]{:S(2)}) async-start(bf16[4,256,768]{2,1,0:T(8,128)(2,1)} %get-tuple-element.109), calls=%async_computation.4 | async-start | bytes 3145728 | tf_op jit(solution)/shard_map/all_to_all | solution.py:655
  252.3 9.6 %collective-permute-start.20 = (bf16[96,1408]{1,0:T(8,128)(2,1)}, bf16[96,1408]{1,0:T(8,128)(2,1)}, u32[]{:S(2)}, u32[]{:S(2)}) collective-permute-start(bf16[96,1408]{1,0:T(8,128)(2,1)} %get-tuple-element.121), channel_id=1, source_target_pairs={{0,1},{1,0},{2,3},{3,2},{4,5},{5,4},{6,7},{7,6},{8,9},{9,8},{10,11... | collective-permute-start | bytes 811016 | tf_op jit(solution)/shard_map/ppermute | solution.py:646
  252.3 15.0 %collective-permute-start.21 = (bf16[96,1408]{1,0:T(8,128)(2,1)}, bf16[96,1408]{1,0:T(8,128)(2,1)}, u32[]{:S(2)}, u32[]{:S(2)}) collective-permute-start(bf16[96,1408]{1,0:T(8,128)(2,1)} %get-tuple-element.123), channel_id=1, source_target_pairs={{0,2},{1,3},{2,0},{3,1},{4,6},{5,7},{6,4},{7,5},{8,10},{9,11},{10,... | collective-permute-start | bytes 811016 | tf_op jit(solution)/shard_map/ppermute | solution.py:646
  252.3 15.0 %collective-permute-start.22 = (bf16[96,1408]{1,0:T(8,128)(2,1)}, bf16[96,1408]{1,0:T(8,128)(2,1)}, u32[]{:S(2)}, u32[]{:S(2)}) collective-permute-start(bf16[96,1408]{1,0:T(8,128)(2,1)} %get-tuple-element.122), channel_id=1, source_target_pairs={{0,3},{1,2},{2,1},{3,0},{4,7},{5,6},{6,5},{7,4},{8,11},{9,10},{10,... | collective-permute-start | bytes 811016 | tf_op jit(solution)/shard_map/ppermute | solution.py:646
  286.5 8.4 %collective-permute-start.23 = (bf16[24,2176]{1,0:T(8,128)(2,1)S(1)}, bf16[24,2176]{1,0:T(8,128)(2,1)S(1)}, u32[]{:S(2)}, u32[]{:S(2)}) collective-permute-start(bf16[24,2176]{1,0:T(8,128)(2,1)S(1)} %get-tuple-element.126), channel_id=1, source_target_pairs={{0,4},{1,5},{2,6},{3,7},{4,0},{5,1},{6,2},{7,3},{8,12},{9,13},{10,... | collective-permute-start | bytes 313352 | tf_op jit(solution)/shard_map/ppermute | solution.py:643
  287.6 11.0 %collective-permute-start.24 = (bf16[24,2176]{1,0:T(8,128)(2,1)S(1)}, bf16[24,2176]{1,0:T(8,128)(2,1)S(1)}, u32[]{:S(2)}, u32[]{:S(2)}) collective-permute-start(bf16[24,2176]{1,0:T(8,128)(2,1)S(1)} %get-tuple-element.125), channel_id=1, source_target_pairs={{0,8},{1,9},{2,10},{3,11},{4,12},{5,13},{6,14},{7,15},{8,0},{9,1},... | collective-permute-start | bytes 313352 | tf_op jit(solution)/shard_map/ppermute | solution.py:643
  289.3 9.2 %collective-permute-start.25 = (bf16[24,2176]{1,0:T(8,128)(2,1)S(1)}, bf16[24,2176]{1,0:T(8,128)(2,1)S(1)}, u32[]{:S(2)}, u32[]{:S(2)}) collective-permute-start(bf16[24,2176]{1,0:T(8,128)(2,1)S(1)} %get-tuple-element.124), channel_id=1, source_target_pairs={{0,12},{1,13},{2,14},{3,15},{4,8},{5,9},{6,10},{7,11},{8,4},{9,5},... | collective-permute-start | bytes 313352 | tf_op jit(solution)/shard_map/ppermute | solution.py:643
  (30 other events, 244.3 us)

commit v2 on v1

--- a/solution.py
+++ b/solution.py
@@ -565,7 +565,7 @@
         in_specs=[pl.BlockSpec(memory_space=pltpu.SMEM)]
         + [pl.BlockSpec(memory_space=pltpu.VMEM)] * (12 + TP + len(kv_grads)),
         scratch_shapes=[pltpu.VMEM((3 * span, width), low), pltpu.VMEM((3 * span, count), low)],
-        compiler_params=pltpu.CompilerParams(vmem_limit_bytes=VMEM),
+        compiler_params=pltpu.CompilerParams(vmem_limit_bytes=36 * 2**20),
         cost_estimate=pl.CostEstimate(
             flops=50 * width * span * count, bytes_accessed=16 * count * width, transcendentals=count
         ),

time: 307 us -> 299 us (0.974)
  waiting for transfers between devices: 89.5 us -> 81.7 us
  Pallas kernels: 85.8 us -> 88.9 us
    pallas_call x2, Pallas kernels: 43.9 us -> 53.3 us  [attention_call(): pl.pallas_call(functools.partial(kernel, heads, groups, runs), out_shape=...]
    pallas_call x1, Pallas kernels: 11.8 us -> 5.48 us  [finish(): pl.pallas_call(functools.partial(finish_kernel, heads), out_shape=(jax.Sh...]
    ppermute x12, waiting for transfers between devices: 20.2 us -> 15.8 us  [over_parts(): lax.ppermute(value, 'blk', [(i, i ^ away * groups) for i in range(members)])]
  transfers between devices with their start and end apart: 31 -> 31, of which waited for: 15 -> 15; matrix products, arithmetic and copies ran while one was open for 10% -> 10% of each run, Pallas kernels for 24% -> 28%
where the time goes in v2:
time: 299 us; the launch traced here: 297 us
  Pallas kernels  88.9 us (30%)
  waiting for transfers between devices  81.7 us (27%)
  starting transfers between devices  78.5 us (26%)
  local copies, waits for them, and re-layouts  25.1 us (8%)
  other arithmetic  16.2 us (5%)
  matrix products  3.47 us (1%)
  between operations  3.23 us (1%)
    pallas_call x2, Pallas kernels, attention_call(): pl.pallas_call(functools.partial(kernel, heads, groups, runs), out_shape=...  53.3 us
    all_to_all x5, waiting for transfers between devices, swapped(): lax.all_to_all(value, 'blk', 0, 0, axis_index_groups=lines, tiled=True)  41.5 us
    ppermute x10, starting transfers between devices, over_groups(): return lax.ppermute(value, 'blk', [(i, i ^ away) for i in range(members)])  28.8 us
    ppermute x12, starting transfers between devices, over_parts(): lax.ppermute(value, 'blk', [(i, i ^ away * groups) for i in range(members)])  26.5 us
    ppermute x10, waiting for transfers between devices, over_groups(): return lax.ppermute(value, 'blk', [(i, i ^ away) for i in range(members)])  22.9 us
    all_to_all x5, starting transfers between devices, swapped(): lax.all_to_all(value, 'blk', 0, 0, axis_index_groups=lines, tiled=True)  22.4 us
    pallas_call x1, Pallas kernels, feed(): pl.pallas_call(functools.partial(feed_kernel, heads), out_shape=(jax.Shap...  19 us
    ppermute x12, waiting for transfers between devices, over_parts(): lax.ppermute(value, 'blk', [(i, i ^ away * groups) for i in range(members)])  15.8 us
  transfers between devices with their start and end apart: 31, of which 15 were waited for; matrix products, arithmetic and copies ran while one was open for 10% of the time, Pallas kernels for 28%

profile of v2, /device:TPU:0, one launch (start us, length us, event | category | flops | bytes accessed | tf_op | source)
XLA Modules:
  0.0 297.1 jit_solution(12131167395474086672)
XLA Ops:
  5.3 6.3 %all-to-all-start = ((bf16[4,24,2176]{2,1,0:T(8,128)(2,1)}), bf16[4,24,2176]{2,1,0:T(8,128)(2,1)S(1)}, u32[]{:S(2)}, u32[]{:S(2)}) async-start(bf16[4,24,2176]{2,1,0:T(8,128)(2,1)} %concatenate.29), calls=%async_computation | async-start | bytes 835584 | tf_op jit(solution)/shard_map/all_to_all | solution.py:655
  15.9 2.4 iota_compare_fusion.3
  18.3 5.4 %all-to-all-done = bf16[4,24,2176]{2,1,0:T(8,128)(2,1)S(1)} async-done(((bf16[4,24,2176]{2,1,0:T(8,128)(2,1)}), bf16[4,24,2176]{2,1,0:T(8,128)(2,1)S(1)}, u32[]{:S(2)}, u32[]{:S(2)}) %all-to-all-start) | async-done | bytes 417824 | tf_op jit(solution)/shard_map/all_to_all | solution.py:655
  24.5 3.7 %all-to-all-start.1 = ((bf16[4,96,640]{2,1,0:T(8,128)(2,1)}), bf16[4,96,640]{2,1,0:T(8,128)(2,1)S(1)}, u32[]{:S(2)}, u32[]{:S(2)}) async-start(bf16[4,96,640]{2,1,0:T(8,128)(2,1)} %broadcast_in_dim.73), calls=%async_computation.1 | async-start | bytes 983040 | tf_op jit(solution)/shard_map/all_to_all | solution.py:655
  29.3 3.2 %collective-permute-start.2 = (bf16[256,768]{1,0:T(8,128)(2,1)S(1)}, bf16[256,768]{1,0:T(8,128)(2,1)S(1)}, u32[]{:S(2)}, u32[]{:S(2)}) collective-permute-start(bf16[256,768]{1,0:T(8,128)(2,1)S(1)} %select_bitcast_fusion.refs_0_.x_ref), channel_id=1, source_target_pairs={{0,12},{1,13},{2,14},{3,15},{4,8},{5,9},{6,10},{7,11},{8,4},{9,5},... | collective-permute-start | bytes 1179656 | tf_op jit(solution)/shard_map/ppermute | solution.py:643
  36.1 3.8 %all-to-all-start.2 = ((bf16[4,96,2304]{2,1,0:T(8,128)(2,1)}), bf16[4,96,2304]{2,1,0:T(8,128)(2,1)S(1)}, u32[]{:S(2)}, u32[]{:S(2)}) async-start(bf16[4,96,2304]{2,1,0:T(8,128)(2,1)} %broadcast_in_dim.78), calls=%async_computation.2 | async-start | bytes 3538944 | tf_op jit(solution)/shard_map/all_to_all | solution.py:655
  41.8 16.3 %all-to-all-done.2 = bf16[4,96,2304]{2,1,0:T(8,128)(2,1)S(1)} async-done(((bf16[4,96,2304]{2,1,0:T(8,128)(2,1)}), bf16[4,96,2304]{2,1,0:T(8,128)(2,1)S(1)}, u32[]{:S(2)}, u32[]{:S(2)}) %all-to-all-start.2) | async-done | bytes 1769504 | tf_op jit(solution)/shard_map/all_to_all | solution.py:655
  59.2 5.5 %collective-permute-start.4 = (bf16[256,768]{1,0:T(8,128)(2,1)}, bf16[256,768]{1,0:T(8,128)(2,1)S(1)}, u32[]{:S(2)}, u32[]{:S(2)}) collective-permute-start(bf16[256,768]{1,0:T(8,128)(2,1)} %bitcast.113), channel_id=1, source_target_pairs={{0,4},{1,5},{2,6},{3,7},{4,0},{5,1},{6,2},{7,3},{8,12},{9,13},{10,... | collective-permute-start | bytes 1179656 | tf_op jit(solution)/shard_map/ppermute | solution.py:643
  64.7 7.9 %prepare.1 = (bf16[192,1024]{1,0:T(8,128)(2,1)}, bf16[384,1024]{1,0:T(8,128)(2,1)}, bf16[1024,768]{1,0:T(8,128)(2,1)}, bf16[1024,768]{1,0:T(8,128)(2,1)}, bf16[576,768]{1,0:T(8,128)(2,1)}, /*index=5*/f32[64,768]{1,0:T(8,128)}) custom-call(bf16[768,768]{1,0:T(8,128)(2,1)} %get-tuple-element.139.order_ref, s32[576,1]{1,0:T(8,128)} %copy.86.source_ref, ...), custom_call_target="tpu_custom_call" | custom-call | flops 7549747200 | bytes 12582912 | tf_op jit(solution)/shard_map/prepare/pallas_call | solution.py:350
  72.6 2.6 collective-permute-start.10
  75.7 5.7 %collective-permute-done.4.refs_5_ = bf16[256,768]{1,0:T(8,128)(2,1)S(1)} collective-permute-done((bf16[256,768]{1,0:T(8,128)(2,1)}, bf16[256,768]{1,0:T(8,128)(2,1)S(1)}, u32[]{:S(2)}, u32[]{:S(2)}) %collective-permute-start.4) | collective-permute-done | bytes 393248 | tf_op jit(solution)/shard_map/ppermute | solution.py:643
  89.9 6.5 %collective-permute-done.6.refs_7_ = bf16[256,768]{1,0:T(8,128)(2,1)S(1)} collective-permute-done((bf16[256,768]{1,0:T(8,128)(2,1)S(1)}, bf16[256,768]{1,0:T(8,128)(2,1)S(1)}, u32[]{:S(2)}, u32[]{:S(2)}) %collective-permute-start.6) | collective-permute-done | bytes 393248 | tf_op jit(solution)/shard_map/ppermute | solution.py:643
  97.1 19.0 %feed.1 = (bf16[192,1024]{1,0:T(8,128)(2,1)}, bf16[192,768]{1,0:T(8,128)(2,1)}, f32[1024,768]{1,0:T(8,128)}, f32[1024,768]{1,0:T(8,128)}, f32[8,768]{1,0:T(8,128...) custom-call(s32[1]{0:T(128)} %bitcast.30.part_ref, bf16[768,768]{1,0:T(8,128)(2,1)} %get-tuple-element.139.order_ref, ...), custom_call_target="tpu_custom_call" | custom-call | tf_op jit(solution)/shard_map/feed/pallas_call | solution.py:432
  119.2 2.6 add_convert_fusion
  121.8 3.5 %all-to-all-start.3 = ((bf16[4,96,1536]{2,1,0:T(8,128)(2,1)}), bf16[4,96,1536]{2,1,0:T(8,128)(2,1)S(1)}, u32[]{:S(2)}, u32[]{:S(2)}) async-start(bf16[4,96,1536]{2,1,0:T(8,128)(2,1)} %bitcast.35), calls=%async_computation.3 | async-start | bytes 2359296 | tf_op jit(solution)/shard_map/all_to_all | solution.py:655
  125.3 23.2 %attend.1 = (bf16[192,1024]{1,0:T(8,128)(2,1)}, bf16[4096,384]{1,0:T(8,128)(2,1)}, bf16[384,4096]{1,0:T(8,128)(2,1)}, f32[8,1024]{1,0:T(8,128)}, f32[8,1024]{1,0...) custom-call(s32[8]{0:T(128)} %copy-done.35, ...), custom_call_target="tpu_custom_call" | custom-call | flops 37748736000 | bytes 6291456 | tf_op jit(solution)/shard_map/attend/pallas_call | solution.py:228
  148.5 6.9 %collective-permute-start.11 = (bf16[256,768]{1,0:T(8,128)(2,1)}, bf16[256,768]{1,0:T(8,128)(2,1)S(1)}, u32[]{:S(2)}, u32[]{:S(2)}) collective-permute-start(bf16[256,768]{1,0:T(8,128)(2,1)} %get-tuple-element.80), channel_id=1, source_target_pairs={{0,4},{1,5},{2,6},{3,7},{4,0},{5,1},{6,2},{7,3},{8,12},{9,13},{10,... | collective-permute-start | bytes 1179656 | tf_op jit(solution)/shard_map/ppermute | solution.py:643
  157.9 30.2 %attend_back.1 = (f32[192,1024]{1,0:T(8,128)}, bf16[2,384,512]{2,1,0:T(8,128)(2,1)}, bf16[2,384,512]{2,1,0:T(8,128)(2,1)}, bf16[2,384,512]{2,1,0:T(8,128)(2,1)}, bf16[2,384,512]{2,1,0:T(8,128)(2,1)}) custom-call(s32[8]{0:T(128)} %copy-done.35, s32[8]{0:T(128)} %select_reduce_fusion.q_order_ref, s32[32]{0:T(128)} %reshape_reshape.3.k_runs_ref, ...), custom_call_target="tpu_custom_call" | custom-call | flops 37748736000 | bytes 6291456 | tf_op jit(solution)/shard_map/attend_back/pallas_call | solution.py:228
  189.2 3.1 %collective-permute-start.17 = (bf16[2,384,512]{2,1,0:T(8,128)(2,1)}, bf16[2,384,512]{2,1,0:T(8,128)(2,1)S(1)}, u32[]{:S(2)}, u32[]{:S(2)}) collective-permute-start(bf16[2,384,512]{2,1,0:T(8,128)(2,1)} %get-tuple-element.108), channel_id=1, source_target_pairs={{0,1},{1,0},{2,3},{3,2},{4,5},{5,4},{6,7},{7,6},{8,9},{9,8},{10,11... | collective-permute-start | bytes 2359304 | tf_op jit(solution)/shard_map/ppermute | solution.py:646
  192.4 6.4 %collective-permute-start.15 = (bf16[2,384,512]{2,1,0:T(8,128)(2,1)}, bf16[2,384,512]{2,1,0:T(8,128)(2,1)}, u32[]{:S(2)}, u32[]{:S(2)}) collective-permute-start(bf16[2,384,512]{2,1,0:T(8,128)(2,1)} %get-tuple-element.106), channel_id=1, source_target_pairs={{0,2},{1,3},{2,0},{3,1},{4,6},{5,7},{6,4},{7,5},{8,10},{9,11},{10,... | collective-permute-start | bytes 2359304 | tf_op jit(solution)/shard_map/ppermute | solution.py:646
  201.6 3.5 %convolution_convert_fusion.merge_ref = bf16[768,768]{1,0:T(8,128)(2,1)} fusion(bf16[192,1024]{1,0:T(8,128)(2,1)} %get-tuple-element.104, bf16[256,768]{1,0:T(8,128)(2,1)} %copy-done.30, bf16[256,768]{1,0:T(8,128)(2,1)} %copy-done.29, bf16[256,768]{1,0:T(8,128)(2,1)} %copy-done.28, bf16[256,768]{1,0:T(8,128)(2,1)S(1)} %bitcast.118, ...), kind=kOutput, calls=%fused_computation.20 | convolution fusion | flops 535511040 | bytes 3293188 | tf_op jit(solution)/shard_map/dot_general | solution.py:27
  206.6 8.9 %collective-permute-start.18 = (bf16[1,384,512]{2,1,0:T(8,128)(2,1)S(1)}, bf16[1,384,512]{2,1,0:T(8,128)(2,1)S(1)}, u32[]{:S(2)}, u32[]{:S(2)}) collective-permute-start(bf16[1,384,512]{2,1,0:T(8,128)(2,1)S(1)} %slice.227), channel_id=1, source_target_pairs={{0,2},{1,3},{2,0},{3,1},{4,6},{5,7},{6,4},{7,5},{8,10},{9,11},{10,... | collective-permute-start | bytes 1179656 | tf_op jit(solution)/shard_map/ppermute | solution.py:646
  219.6 4.8 %collective-permute-done.18 = bf16[1,384,512]{2,1,0:T(8,128)(2,1)S(1)} collective-permute-done((bf16[1,384,512]{2,1,0:T(8,128)(2,1)S(1)}, bf16[1,384,512]{2,1,0:T(8,128)(2,1)S(1)}, u32[]{:S(2)}, u32[]{:S(2)}) %collective-permute-start.18) | collective-permute-done | bytes 393248 | tf_op jit(solution)/shard_map/ppermute | solution.py:646
  224.4 4.3 %collective-permute-done.16 = bf16[1,384,512]{2,1,0:T(8,128)(2,1)S(1)} collective-permute-done((bf16[1,384,512]{2,1,0:T(8,128)(2,1)S(1)}, bf16[1,384,512]{2,1,0:T(8,128)(2,1)S(1)}, u32[]{:S(2)}, u32[]{:S(2)}) %collective-permute-start.16) | collective-permute-done | bytes 393248 | tf_op jit(solution)/shard_map/ppermute | solution.py:646
  228.8 5.5 %finish.1 = (bf16[384,1408]{1,0:T(8,128)(2,1)S(1)}, bf16[384,1408]{1,0:T(8,128)(2,1)S(1)}, bf16[4,256,768]{2,1,0:T(8,128)(2,1)}) custom-call(s32[1]{0:T(128)} %bitcast.30.part_ref, bf16[768,768]{1,0:T(8,128)(2,1)S(1)} %copy-done, s32[768,1]{1,0:T(8,128)S(1)} %fusion.32.place_ref, s32[1,576]{1,0:T(1,128)S(1)} %fusion.61.source_ref, f32[8,1024]{1,0:T(8,128)S(1)} %copy-done.10, ...), custom_call_target="tpu_custom_call" | custom-call | flops 7549747200 | bytes 12582912 | tf_op jit(solution)/shard_map/finish/pallas_call | solution.py:558
  235.0 5.1 %all-to-all-start.4 = ((bf16[4,256,768]{2,1,0:T(8,128)(2,1)}), bf16[4,256,768]{2,1,0:T(8,128)(2,1)}, u32[]{:S(2)}, u32[]{:S(2)}) async-start(bf16[4,256,768]{2,1,0:T(8,128)(2,1)} %get-tuple-element.109), calls=%async_computation.4 | async-start | bytes 3145728 | tf_op jit(solution)/shard_map/all_to_all | solution.py:655
  247.2 5.8 %collective-permute-done.20 = bf16[96,1408]{1,0:T(8,128)(2,1)S(1)} collective-permute-done((bf16[96,1408]{1,0:T(8,128)(2,1)}, bf16[96,1408]{1,0:T(8,128)(2,1)S(1)}, u32[]{:S(2)}, u32[]{:S(2)}) %collective-permute-start.20) | collective-permute-done | bytes 270368 | tf_op jit(solution)/shard_map/ppermute | solution.py:646
  253.1 6.5 %collective-permute-done.21 = bf16[96,1408]{1,0:T(8,128)(2,1)S(1)} collective-permute-done((bf16[96,1408]{1,0:T(8,128)(2,1)}, bf16[96,1408]{1,0:T(8,128)(2,1)S(1)}, u32[]{:S(2)}, u32[]{:S(2)}) %collective-permute-start.21) | collective-permute-done | bytes 270368 | tf_op jit(solution)/shard_map/ppermute | solution.py:646
  260.8 17.6 %all-to-all-done.4.slopes_ref = bf16[4,256,768]{2,1,0:T(8,128)(2,1)} async-done(((bf16[4,256,768]{2,1,0:T(8,128)(2,1)}), bf16[4,256,768]{2,1,0:T(8,128)(2,1)}, u32[]{:S(2)}, u32[]{:S(2)}) %all-to-all-start.4) | async-done | bytes 1572896 | tf_op jit(solution)/shard_map/all_to_all | solution.py:655
  279.4 2.4 collective-permute-start.24
  283.8 3.2 %tokens_gradient.1 = f32[256,768]{1,0:T(8,128)} custom-call(bf16[256,768]{1,0:T(8,128)(2,1)} %copy-done.1, bf16[256,768]{1,0:T(8,128)(2,1)} %bitcast.116, bf16[4,256,768]{2,1,0:T(8,128)(2,1)} %all-to-all-done.4.slopes_ref), custom_call_target="tpu_custom_call" | custom-call | tf_op jit(solution)/shard_map/tokens_gradient/pallas_call | solution.py:604
  287.0 3.6 %collective-permute-done.24 = bf16[24,2176]{1,0:T(8,128)(2,1)S(1)} collective-permute-done((bf16[24,2176]{1,0:T(8,128)(2,1)S(1)}, bf16[24,2176]{1,0:T(8,128)(2,1)S(1)}, u32[]{:S(2)}, u32[]{:S(2)}) %collective-permute-start.24) | collective-permute-done | bytes 104480 | tf_op jit(solution)/shard_map/ppermute | solution.py:643
  (255 shorter events, 58.7 us)
Async XLA Ops:
  5.3 18.4 %all-to-all-start = ((bf16[4,24,2176]{2,1,0:T(8,128)(2,1)}), bf16[4,24,2176]{2,1,0:T(8,128)(2,1)S(1)}, u32[]{:S(2)}, u32[]{:S(2)}) async-start(bf16[4,24,2176]{2,1,0:T(8,128)(2,1)} %concatenate.29), calls=%async_computation | async-start | bytes 835584 | tf_op jit(solution)/shard_map/all_to_all | solution.py:655
  13.5 45.6 %collective-permute-start = (bf16[256,768]{1,0:T(8,128)(2,1)S(1)}, bf16[256,768]{1,0:T(8,128)(2,1)S(1)}, u32[]{:S(2)}, u32[]{:S(2)}) collective-permute-start(bf16[256,768]{1,0:T(8,128)(2,1)S(1)} %select_bitcast_fusion.refs_0_.x_ref), channel_id=1, source_target_pairs={{0,4},{1,5},{2,6},{3,7},{4,0},{5,1},{6,2},{7,3},{8,12},{9,13},{10,... | collective-permute-start | bytes 1179656 | tf_op jit(solution)/shard_map/ppermute | solution.py:643
  24.5 10.1 %all-to-all-start.1 = ((bf16[4,96,640]{2,1,0:T(8,128)(2,1)}), bf16[4,96,640]{2,1,0:T(8,128)(2,1)S(1)}, u32[]{:S(2)}, u32[]{:S(2)}) async-start(bf16[4,96,640]{2,1,0:T(8,128)(2,1)} %broadcast_in_dim.73), calls=%async_computation.1 | async-start | bytes 983040 | tf_op jit(solution)/shard_map/all_to_all | solution.py:655
  29.3 29.9 %collective-permute-start.1 = (bf16[256,768]{1,0:T(8,128)(2,1)S(1)}, bf16[256,768]{1,0:T(8,128)(2,1)S(1)}, u32[]{:S(2)}, u32[]{:S(2)}) collective-permute-start(bf16[256,768]{1,0:T(8,128)(2,1)S(1)} %select_bitcast_fusion.refs_0_.x_ref), channel_id=1, source_target_pairs={{0,8},{1,9},{2,10},{3,11},{4,12},{5,13},{6,14},{7,15},{8,0},{9,1},... | collective-permute-start | bytes 1179656 | tf_op jit(solution)/shard_map/ppermute | solution.py:643
  29.3 29.9 %collective-permute-start.2 = (bf16[256,768]{1,0:T(8,128)(2,1)S(1)}, bf16[256,768]{1,0:T(8,128)(2,1)S(1)}, u32[]{:S(2)}, u32[]{:S(2)}) collective-permute-start(bf16[256,768]{1,0:T(8,128)(2,1)S(1)} %select_bitcast_fusion.refs_0_.x_ref), channel_id=1, source_target_pairs={{0,12},{1,13},{2,14},{3,15},{4,8},{5,9},{6,10},{7,11},{8,4},{9,5},... | collective-permute-start | bytes 1179656 | tf_op jit(solution)/shard_map/ppermute | solution.py:643
  36.1 22.0 %all-to-all-start.2 = ((bf16[4,96,2304]{2,1,0:T(8,128)(2,1)}), bf16[4,96,2304]{2,1,0:T(8,128)(2,1)S(1)}, u32[]{:S(2)}, u32[]{:S(2)}) async-start(bf16[4,96,2304]{2,1,0:T(8,128)(2,1)} %broadcast_in_dim.78), calls=%async_computation.2 | async-start | bytes 3538944 | tf_op jit(solution)/shard_map/all_to_all | solution.py:655
  41.4 23.3 %collective-permute-start.3 = (bf16[384,640]{1,0:T(8,128)(2,1)}, bf16[384,640]{1,0:T(8,128)(2,1)}, u32[]{:S(2)}, u32[]{:S(2)}) collective-permute-start(bf16[384,640]{1,0:T(8,128)(2,1)} %bitcast.125), channel_id=1, source_target_pairs={{0,16},{16,0},{1,17},{17,1},{2,18},{18,2},{3,19},{19,3},{4,20},{20... | collective-permute-start | bytes 1474568 | tf_op jit(solution)/shard_map/ppermute | solution.py:649
  41.7 75.1 %copy-start.35 = (s32[8]{0:T(128)}, s32[8]{0:T(128)S(1)}, u32[]{:S(2)}) copy-start(s32[8]{0:T(128)S(1)} %squeeze.58.q_runs_ref) | copy-start | bytes 100
  58.1 38.2 %collective-permute-start.7 = (bf16[384,2304]{1,0:T(8,128)(2,1)S(1)}, bf16[384,2304]{1,0:T(8,128)(2,1)}, u32[]{:S(2)}, u32[]{:S(2)}) collective-permute-start(bf16[384,2304]{1,0:T(8,128)(2,1)S(1)} %bitcast.109), channel_id=1, source_target_pairs={{0,16},{16,0},{1,17},{17,1},{2,18},{18,2},{3,19},{19,3},{4,20},{20... | collective-permute-start | bytes 5308424 | tf_op jit(solution)/shard_map/ppermute | solution.py:649
  59.2 22.2 %collective-permute-start.4 = (bf16[256,768]{1,0:T(8,128)(2,1)}, bf16[256,768]{1,0:T(8,128)(2,1)S(1)}, u32[]{:S(2)}, u32[]{:S(2)}) collective-permute-start(bf16[256,768]{1,0:T(8,128)(2,1)} %bitcast.113), channel_id=1, source_target_pairs={{0,4},{1,5},{2,6},{3,7},{4,0},{5,1},{6,2},{7,3},{8,12},{9,13},{10,... | collective-permute-start | bytes 1179656 | tf_op jit(solution)/shard_map/ppermute | solution.py:643
  64.7 20.0 %collective-permute-start.5 = (bf16[256,768]{1,0:T(8,128)(2,1)}, bf16[256,768]{1,0:T(8,128)(2,1)S(1)}, u32[]{:S(2)}, u32[]{:S(2)}) collective-permute-start(bf16[256,768]{1,0:T(8,128)(2,1)} %bitcast.114), channel_id=1, source_target_pairs={{0,8},{1,9},{2,10},{3,11},{4,12},{5,13},{6,14},{7,15},{8,0},{9,1},... | collective-permute-start | bytes 1179656 | tf_op jit(solution)/shard_map/ppermute | solution.py:643
  72.6 43.5 %collective-permute-start.10 = (bf16[384,1024]{1,0:T(8,128)(2,1)}, bf16[384,1024]{1,0:T(8,128)(2,1)}, u32[]{:S(2)}, u32[]{:S(2)}) collective-permute-start(bf16[384,1024]{1,0:T(8,128)(2,1)} %get-tuple-element.75.refs_2_), channel_id=1, source_target_pairs={{0,3},{1,2},{2,1},{3,0},{4,7},{5,6},{6,5},{7,4},{8,11},{9,10},{10,... | collective-permute-start | bytes 2359304 | tf_op jit(solution)/shard_map/ppermute | solution.py:646
  75.2 40.9 %collective-permute-start.8 = (bf16[384,1024]{1,0:T(8,128)(2,1)}, bf16[384,1024]{1,0:T(8,128)(2,1)}, u32[]{:S(2)}, u32[]{:S(2)}) collective-permute-start(bf16[384,1024]{1,0:T(8,128)(2,1)} %get-tuple-element.75.refs_2_), channel_id=1, source_target_pairs={{0,1},{1,0},{2,3},{3,2},{4,5},{5,4},{6,7},{7,6},{8,9},{9,8},{10,11... | collective-permute-start | bytes 2359304 | tf_op jit(solution)/shard_map/ppermute | solution.py:646
  81.4 34.7 %collective-permute-start.9 = (bf16[384,1024]{1,0:T(8,128)(2,1)}, bf16[384,1024]{1,0:T(8,128)(2,1)}, u32[]{:S(2)}, u32[]{:S(2)}) collective-permute-start(bf16[384,1024]{1,0:T(8,128)(2,1)} %get-tuple-element.75.refs_2_), channel_id=1, source_target_pairs={{0,2},{1,3},{2,0},{3,1},{4,6},{5,7},{6,4},{7,5},{8,10},{9,11},{10,... | collective-permute-start | bytes 2359304 | tf_op jit(solution)/shard_map/ppermute | solution.py:646
  84.7 11.6 %collective-permute-start.6 = (bf16[256,768]{1,0:T(8,128)(2,1)S(1)}, bf16[256,768]{1,0:T(8,128)(2,1)S(1)}, u32[]{:S(2)}, u32[]{:S(2)}) collective-permute-start(bf16[256,768]{1,0:T(8,128)(2,1)S(1)} %bitcast.117), channel_id=1, source_target_pairs={{0,12},{1,13},{2,14},{3,15},{4,8},{5,9},{6,10},{7,11},{8,4},{9,5},... | collective-permute-start | bytes 1179656 | tf_op jit(solution)/shard_map/ppermute | solution.py:643
  116.1 3.1 %collective-permute-start.14 = (bf16[384,1536]{1,0:T(8,128)(2,1)}, bf16[384,1536]{1,0:T(8,128)(2,1)S(1)}, u32[]{:S(2)}, u32[]{:S(2)}) collective-permute-start(bf16[384,1536]{1,0:T(8,128)(2,1)} %get-tuple-element.87), channel_id=1, source_target_pairs={{0,16},{16,0},{1,17},{17,1},{2,18},{18,2},{3,19},{19,3},{4,20},{20... | collective-permute-start | bytes 3538952 | tf_op jit(solution)/shard_map/ppermute | solution.py:649
  121.8 36.1 %all-to-all-start.3 = ((bf16[4,96,1536]{2,1,0:T(8,128)(2,1)}), bf16[4,96,1536]{2,1,0:T(8,128)(2,1)S(1)}, u32[]{:S(2)}, u32[]{:S(2)}) async-start(bf16[4,96,1536]{2,1,0:T(8,128)(2,1)} %bitcast.35), calls=%async_computation.3 | async-start | bytes 2359296 | tf_op jit(solution)/shard_map/all_to_all | solution.py:655
  148.5 39.5 %collective-permute-start.11 = (bf16[256,768]{1,0:T(8,128)(2,1)}, bf16[256,768]{1,0:T(8,128)(2,1)S(1)}, u32[]{:S(2)}, u32[]{:S(2)}) collective-permute-start(bf16[256,768]{1,0:T(8,128)(2,1)} %get-tuple-element.80), channel_id=1, source_target_pairs={{0,4},{1,5},{2,6},{3,7},{4,0},{5,1},{6,2},{7,3},{8,12},{9,13},{10,... | collective-permute-start | bytes 1179656 | tf_op jit(solution)/shard_map/ppermute | solution.py:643
  155.4 32.6 %collective-permute-start.12 = (bf16[256,768]{1,0:T(8,128)(2,1)}, bf16[256,768]{1,0:T(8,128)(2,1)S(1)}, u32[]{:S(2)}, u32[]{:S(2)}) collective-permute-start(bf16[256,768]{1,0:T(8,128)(2,1)} %get-tuple-element.81), channel_id=1, source_target_pairs={{0,8},{1,9},{2,10},{3,11},{4,12},{5,13},{6,14},{7,15},{8,0},{9,1},... | collective-permute-start | bytes 1179656 | tf_op jit(solution)/shard_map/ppermute | solution.py:643
  155.7 32.3 %collective-permute-start.13 = (bf16[256,768]{1,0:T(8,128)(2,1)}, bf16[256,768]{1,0:T(8,128)(2,1)S(1)}, u32[]{:S(2)}, u32[]{:S(2)}) collective-permute-start(bf16[256,768]{1,0:T(8,128)(2,1)} %get-tuple-element.82), channel_id=1, source_target_pairs={{0,12},{1,13},{2,14},{3,15},{4,8},{5,9},{6,10},{7,11},{8,4},{9,5},... | collective-permute-start | bytes 1179656 | tf_op jit(solution)/shard_map/ppermute | solution.py:643
  189.2 17.1 %collective-permute-start.17 = (bf16[2,384,512]{2,1,0:T(8,128)(2,1)}, bf16[2,384,512]{2,1,0:T(8,128)(2,1)S(1)}, u32[]{:S(2)}, u32[]{:S(2)}) collective-permute-start(bf16[2,384,512]{2,1,0:T(8,128)(2,1)} %get-tuple-element.108), channel_id=1, source_target_pairs={{0,1},{1,0},{2,3},{3,2},{4,5},{5,4},{6,7},{7,6},{8,9},{9,8},{10,11... | collective-permute-start | bytes 2359304 | tf_op jit(solution)/shard_map/ppermute | solution.py:646
  192.4 23.2 %collective-permute-start.15 = (bf16[2,384,512]{2,1,0:T(8,128)(2,1)}, bf16[2,384,512]{2,1,0:T(8,128)(2,1)}, u32[]{:S(2)}, u32[]{:S(2)}) collective-permute-start(bf16[2,384,512]{2,1,0:T(8,128)(2,1)} %get-tuple-element.106), channel_id=1, source_target_pairs={{0,2},{1,3},{2,0},{3,1},{4,6},{5,7},{6,4},{7,5},{8,10},{9,11},{10,... | collective-permute-start | bytes 2359304 | tf_op jit(solution)/shard_map/ppermute | solution.py:646
  206.6 17.8 %collective-permute-start.18 = (bf16[1,384,512]{2,1,0:T(8,128)(2,1)S(1)}, bf16[1,384,512]{2,1,0:T(8,128)(2,1)S(1)}, u32[]{:S(2)}, u32[]{:S(2)}) collective-permute-start(bf16[1,384,512]{2,1,0:T(8,128)(2,1)S(1)} %slice.227), channel_id=1, source_target_pairs={{0,2},{1,3},{2,0},{3,1},{4,6},{5,7},{6,4},{7,5},{8,10},{9,11},{10,... | collective-permute-start | bytes 1179656 | tf_op jit(solution)/shard_map/ppermute | solution.py:646
  217.3 11.4 %collective-permute-start.16 = (bf16[1,384,512]{2,1,0:T(8,128)(2,1)S(1)}, bf16[1,384,512]{2,1,0:T(8,128)(2,1)S(1)}, u32[]{:S(2)}, u32[]{:S(2)}) collective-permute-start(bf16[1,384,512]{2,1,0:T(8,128)(2,1)S(1)} %slice.228), channel_id=1, source_target_pairs={{0,1},{1,0},{2,3},{3,2},{4,5},{5,4},{6,7},{7,6},{8,9},{9,8},{10,11... | collective-permute-start | bytes 1179656 | tf_op jit(solution)/shard_map/ppermute | solution.py:646
  234.3 5.7 %collective-permute-start.19 = (bf16[384,1408]{1,0:T(8,128)(2,1)S(1)}, bf16[384,1408]{1,0:T(8,128)(2,1)S(1)}, u32[]{:S(2)}, u32[]{:S(2)}) collective-permute-start(bf16[384,1408]{1,0:T(8,128)(2,1)S(1)} %get-tuple-element.111), channel_id=1, source_target_pairs={{0,16},{16,0},{1,17},{17,1},{2,18},{18,2},{3,19},{19,3},{4,20},{20... | collective-permute-start | bytes 3244040 | tf_op jit(solution)/shard_map/ppermute | solution.py:649
  235.0 43.5 %all-to-all-start.4 = ((bf16[4,256,768]{2,1,0:T(8,128)(2,1)}), bf16[4,256,768]{2,1,0:T(8,128)(2,1)}, u32[]{:S(2)}, u32[]{:S(2)}) async-start(bf16[4,256,768]{2,1,0:T(8,128)(2,1)} %get-tuple-element.109), calls=%async_computation.4 | async-start | bytes 3145728 | tf_op jit(solution)/shard_map/all_to_all | solution.py:655
  243.5 9.5 %collective-permute-start.20 = (bf16[96,1408]{1,0:T(8,128)(2,1)}, bf16[96,1408]{1,0:T(8,128)(2,1)S(1)}, u32[]{:S(2)}, u32[]{:S(2)}) collective-permute-start(bf16[96,1408]{1,0:T(8,128)(2,1)} %get-tuple-element.121), channel_id=1, source_target_pairs={{0,1},{1,0},{2,3},{3,2},{4,5},{5,4},{6,7},{7,6},{8,9},{9,8},{10,11... | collective-permute-start | bytes 811016 | tf_op jit(solution)/shard_map/ppermute | solution.py:646
  245.3 14.3 %collective-permute-start.21 = (bf16[96,1408]{1,0:T(8,128)(2,1)}, bf16[96,1408]{1,0:T(8,128)(2,1)S(1)}, u32[]{:S(2)}, u32[]{:S(2)}) collective-permute-start(bf16[96,1408]{1,0:T(8,128)(2,1)} %get-tuple-element.123), channel_id=1, source_target_pairs={{0,2},{1,3},{2,0},{3,1},{4,6},{5,7},{6,4},{7,5},{8,10},{9,11},{10,... | collective-permute-start | bytes 811016 | tf_op jit(solution)/shard_map/ppermute | solution.py:646
  245.7 14.0 %collective-permute-start.22 = (bf16[96,1408]{1,0:T(8,128)(2,1)}, bf16[96,1408]{1,0:T(8,128)(2,1)}, u32[]{:S(2)}, u32[]{:S(2)}) collective-permute-start(bf16[96,1408]{1,0:T(8,128)(2,1)} %get-tuple-element.122), channel_id=1, source_target_pairs={{0,3},{1,2},{2,1},{3,0},{4,7},{5,6},{6,5},{7,4},{8,11},{9,10},{10,... | collective-permute-start | bytes 811016 | tf_op jit(solution)/shard_map/ppermute | solution.py:646
  278.6 8.4 %collective-permute-start.23 = (bf16[24,2176]{1,0:T(8,128)(2,1)S(1)}, bf16[24,2176]{1,0:T(8,128)(2,1)S(1)}, u32[]{:S(2)}, u32[]{:S(2)}) collective-permute-start(bf16[24,2176]{1,0:T(8,128)(2,1)S(1)} %get-tuple-element.126), channel_id=1, source_target_pairs={{0,4},{1,5},{2,6},{3,7},{4,0},{5,1},{6,2},{7,3},{8,12},{9,13},{10,... | collective-permute-start | bytes 313352 | tf_op jit(solution)/shard_map/ppermute | solution.py:643
  279.4 11.2 %collective-permute-start.24 = (bf16[24,2176]{1,0:T(8,128)(2,1)S(1)}, bf16[24,2176]{1,0:T(8,128)(2,1)S(1)}, u32[]{:S(2)}, u32[]{:S(2)}) collective-permute-start(bf16[24,2176]{1,0:T(8,128)(2,1)S(1)} %get-tuple-element.125), channel_id=1, source_target_pairs={{0,8},{1,9},{2,10},{3,11},{4,12},{5,13},{6,14},{7,15},{8,0},{9,1},... | collective-permute-start | bytes 313352 | tf_op jit(solution)/shard_map/ppermute | solution.py:643
  281.8 8.8 %collective-permute-start.25 = (bf16[24,2176]{1,0:T(8,128)(2,1)S(1)}, bf16[24,2176]{1,0:T(8,128)(2,1)S(1)}, u32[]{:S(2)}, u32[]{:S(2)}) collective-permute-start(bf16[24,2176]{1,0:T(8,128)(2,1)S(1)} %get-tuple-element.124), channel_id=1, source_target_pairs={{0,12},{1,13},{2,14},{3,15},{4,8},{5,9},{6,10},{7,11},{8,4},{9,5},... | collective-permute-start | bytes 313352 | tf_op jit(solution)/shard_map/ppermute | solution.py:643
  (44 other events, 428.1 us)
